TPU v7x, 512 devices: a whole 4x8x8 slice. The times are simulated.
512 devices in a mesh: slab: 16 (over x_lo, z), sub: 32 (over y, x_hi, core).
Axes of the slice: x: 4 (x_hi: 2, x_lo: 2; x = x_hi * 2 + x_lo), y: 8, z: 8, core: 2. Of those that a mesh axis runs over, the one named last changes fastest.
Arguments:
- positions: float32 [3, 131072], P(None, ('slab', 'sub')), may hold values from 0 to 1
- features: bfloat16 [64, 131072], P(None, ('slab', 'sub')), may hold values from -6 to 6
- neighbours: int32 [16, 131072], P(None, ('slab', 'sub')), may hold values from 0 to 383
- miller: int32 [3, 2048], replicated, may hold values from -4 to 4
- filter_weights: float32 [2048, 64], replicated, may hold values from -6 to 6
- energy_weights: float32 [64], replicated, may hold values from -0.06 to 0.06
Outputs:
- updated: float32 [64, 131072], P(None, ('slab', 'sub'))
- forces: float32 [3, 131072], P(None, ('slab', 'sub'))
All inputs are finite; a program needn't handle non-finite values.
Results may differ from a plain program's by a relative error of at most 0.0005.
Values sent between devices are 32-bit elements; how exact they have to be, the bound alone decides.
A program may use at most 64 MiB of HBM per device.

v0:
```python
import math

import jax
import jax.numpy as jnp
from jax import lax
from jax.sharding import PartitionSpec as P

GHOST = 64


TWO_PI = 2.0 * math.pi
BETA = 1.0
SHORT_SCALE = 0.25
KBLOCK = 256


def extended_2(value, sides, width):
    for axis, dim in sides:
        size, length = (lax.axis_size(axis), value.shape[dim])
        up = [(i, (i + 1) % size) for i in range(size)]
        down = [(j, i) for i, j in up]
        last = lax.slice_in_dim(value, length - width, length, axis=dim)
        leading = lax.slice_in_dim(value, 0, width, axis=dim)
        before = lax.ppermute(last, axis, up)
        after = lax.ppermute(leading, axis, down)
        value = jnp.concatenate([before, value, after], axis=dim)
    return value


def exact_dot(left, right):
    return jnp.dot(left, right, precision=lax.Precision.HIGHEST, preferred_element_type=jnp.float32)


def phase_pair(positions, miller_block):
    miller_float = miller_block.astype(jnp.float32)
    angle = TWO_PI * (
        miller_float[0][:, None] * positions[0][None, :]
        + miller_float[1][:, None] * positions[1][None, :]
        + miller_float[2][:, None] * positions[2][None, :]
    )
    return (jnp.cos(angle), jnp.sin(angle))


def over_kvec(miller, running, update):
    kvec_total = miller.shape[1]
    block_size = min(KBLOCK, kvec_total)

    def advance(carry, block_index):
        first_k = block_index * block_size
        miller_block = lax.dynamic_slice_in_dim(miller, first_k, block_size, 1)
        return update(carry, miller_block, first_k, block_size)

    return lax.scan(advance, running, jnp.arange(kvec_total // block_size, dtype=jnp.int32))


def factor_part(positions, values, miller):

    def update(carry, miller_block, first_k, block_size):
        cosines, sines = phase_pair(positions, miller_block)
        return (
            carry,
            jnp.concatenate([exact_dot(cosines, values.T), exact_dot(sines, values.T)], 1),
        )

    _, stacked = over_kvec(miller, jnp.zeros((), jnp.float32), update)
    return stacked.reshape(miller.shape[1], 2 * values.shape[0])


def long_eval(positions, miller, weighted):
    channels = weighted.shape[1] // 2

    def update(running, miller_block, first_k, block_size):
        cosines, sines = phase_pair(positions, miller_block)
        rows_here = lax.dynamic_slice_in_dim(weighted, first_k, block_size, 0)
        running = (
            running
            + exact_dot(rows_here[:, :channels].T, cosines)
            + exact_dot(rows_here[:, channels:].T, sines)
        )
        return (running, jnp.zeros((), jnp.float32))

    final, _ = over_kvec(miller, jnp.zeros((channels, positions.shape[1]), jnp.float32), update)
    return final


def phase_force(positions, miller, weighted, grads, energy_grad, feat_wide):
    channels = weighted.shape[1] // 2
    paired = jnp.concatenate([energy_grad, feat_wide], 0)

    def update(running, miller_block, first_k, block_size):
        cosines, sines = phase_pair(positions, miller_block)
        rows_w = lax.dynamic_slice_in_dim(weighted, first_k, block_size, 0)
        rows_g = lax.dynamic_slice_in_dim(grads, first_k, block_size, 0)
        real_side = exact_dot(
            jnp.concatenate([rows_w[:, :channels], rows_g[:, :channels]], 1), paired
        )
        imag_side = exact_dot(
            jnp.concatenate([rows_w[:, channels:], rows_g[:, channels:]], 1), paired
        )
        angle_grad = cosines * imag_side - sines * real_side
        running = running + TWO_PI * exact_dot(miller_block.astype(jnp.float32), angle_grad)
        return (running, jnp.zeros((), jnp.float32))

    final, _ = over_kvec(miller, jnp.zeros((3, positions.shape[1]), jnp.float32), update)
    return final


def short_terms(own_pos, ext_pos, ext_feat, neighbours):

    def one_slot(running, index_row):
        near_pos = jnp.take(ext_pos, index_row, axis=1)
        near_feat = jnp.take(ext_feat, index_row, axis=1)
        offset = own_pos - near_pos
        weight = jnp.exp(BETA * (jnp.sum(jnp.cos(TWO_PI * offset), 0) - 3.0))
        return (running + weight[None, :] * near_feat, None)

    empty_sum = jnp.zeros((ext_feat.shape[0], own_pos.shape[1]), jnp.float32)
    summed, _ = lax.scan(one_slot, empty_sum, neighbours)
    return SHORT_SCALE * summed


def short_grad(own_pos, ext_pos, ext_feat, neighbours, energy_grad):

    def one_slot(running, index_row):
        own_acc, ext_acc = running
        near_pos = jnp.take(ext_pos, index_row, axis=1)
        near_feat = jnp.take(ext_feat, index_row, axis=1)
        offset = own_pos - near_pos
        weight = jnp.exp(BETA * (jnp.sum(jnp.cos(TWO_PI * offset), 0) - 3.0))
        weight_grad = SHORT_SCALE * jnp.sum(energy_grad * near_feat, 0)
        force_term = (weight_grad * weight * BETA * -TWO_PI)[None, :] * jnp.sin(TWO_PI * offset)
        own_acc = own_acc + force_term
        ext_acc = ext_acc.at[:, index_row].add(-force_term)
        return ((own_acc, ext_acc), None)

    start_own = jnp.zeros((3, own_pos.shape[1]), jnp.float32)
    start_ext = jnp.zeros((3, ext_pos.shape[1]), jnp.float32)
    (own_acc, ext_acc), _ = lax.scan(one_slot, (start_own, start_ext), neighbours)
    return (own_acc, ext_acc)


def on_device(positions, features, neighbours, miller, filter_weights, energy_weights):
    feat_wide = features.astype(jnp.float32)
    atoms_here = positions.shape[1]
    norm_scale = 1.0 / math.sqrt(
        atoms_here * lax.axis_size("slab") * lax.axis_size("sub") * miller.shape[1]
    )
    partial_value = factor_part(positions, feat_wide, miller)
    factor = lax.psum(partial_value, ("slab", "sub"))
    stacked = jnp.concatenate([positions, feat_wide], 0)
    extended = extended_2(stacked, (("slab", 1),), GHOST)
    ext_pos = extended[:3]
    ext_feat = extended[3:]
    short_part = short_terms(positions, ext_pos, ext_feat, neighbours)
    filter_pair = jnp.concatenate([filter_weights, filter_weights], 1)
    weighted = norm_scale * filter_pair * factor
    long_part = long_eval(positions, miller, weighted)
    updated = feat_wide + short_part + long_part
    squashed = jnp.tanh(updated)
    energy_grad = energy_weights[:, None] * (1.0 - squashed * squashed)
    grad_partial = factor_part(positions, energy_grad, miller)
    grads_sum = lax.psum(grad_partial, ("slab", "sub"))
    own_acc, ext_acc = short_grad(positions, ext_pos, ext_feat, neighbours, energy_grad)
    rim_grads = jnp.concatenate([ext_acc[:, :GHOST], ext_acc[:, GHOST + atoms_here :]], 1)
    returned = extended_2(rim_grads, (("slab", 1),), GHOST)
    grads = norm_scale * filter_pair * grads_sum
    long_grad = phase_force(positions, miller, weighted, grads, energy_grad, feat_wide)
    own_grads = own_acc + ext_acc[:, GHOST : GHOST + atoms_here]
    own_grads = own_grads.at[:, atoms_here - GHOST :].add(returned[:, 3 * GHOST :])
    own_grads = own_grads.at[:, :GHOST].add(returned[:, :GHOST])
    forces = -(long_grad + own_grads)
    return (updated, forces)


def solution(mesh):
    return jax.shard_map(
        on_device,
        mesh=mesh,
        in_specs=(
            P(None, ("slab", "sub")),
            P(None, ("slab", "sub")),
            P(None, ("slab", "sub")),
            P(),
            P(),
            P(),
        ),
        out_specs=(P(None, ("slab", "sub")), P(None, ("slab", "sub"))),
        check_vma=False,
    )
```

profile of v0, /device:TPU:1, one launch (start us, length us, event | category | flops | bytes accessed | tf_op | source)
XLA Modules:
  0.0 838.8 jit_solution(18310382647258361123)
XLA Ops:
  8.1 4.8 collective-permute-start
  12.9 9.5 %collective-permute-start.1 = (f32[67,64]{1,0:T(8,128)S(1)}, f32[67,64]{1,0:T(8,128)S(1)}, u32[]{:S(2)}, u32[]{:S(2)}) collective-permute-start(f32[67,64]{1,0:T(8,128)S(1)} %get-tuple-element.593), channel_id=1, source_target_pairs={{32,0},{64,32},{96,64},{128,96},{160,128},{192,160},{224,192},{256... | collective-permute-start | bytes 51464 | tf_op jit(solution)/shard_map/ppermute | solution.py:25
  22.5 38.6 %while.72 = (s32[]{:T(128)}, f32[8,256,128]{2,1,0:T(8,128)S(1)}, s32[8]{0:T(128)S(1)}, s32[3,2048]{1,0:T(4,128)}, f32[3,256]{1,0:T(4,128)S(1)}, /*index=5*/f32[6...) while((s32[]{:T(128)}, f32[8,256,128]{2,1,0:T(8,128)S(1)}, s32[8]{0:T(128)S(1)}, ...), condition=%wide.region_4.7_spmd, body=%wide.region_3.6_spmd.sunk | while | flops 101483264 | bytes 1079463 | solution.py:53
  24.5 1.4 fusion.145
  25.8 1.4 fusion.144
  30.6 1.4 fusion.144
  35.5 1.4 fusion.144
  40.3 1.4 fusion.144
  45.1 1.4 fusion.144
  49.9 1.4 fusion.144
  54.7 1.4 fusion.144
  59.6 1.4 fusion.144
  64.0 47.7 %while.74 = (s32[]{:T(128)}, f32[64,256]{0,1:T(8,128)S(1)}, s32[16,256]{1,0:T(8,128)}, f32[3,384]{0,1:T(8,128)S(1)}, f32[3,256]{0,1:T(8,128)S(1)}, /*index=5*/f32[64,384]{0,1:T(8,128)S(1)}, s32[]{:T(128)}, s32[]{:T(128)}) while((s32[]{:T(128)}, f32[64,256]{0,1:T(8,128)S(1)}, s32[16,256]{1,0:T(8,128)}, f32[3,384]{0,1:T(8,128)S(1)}, ...), condition=%wide.region_2.0_spmd.clone, body=%wide.region_0.4_spmd.clone.sunk | while | flops 71939 | bytes 357219 | solution.py:118
  111.7 221.3 %all-reduce.3.cloned.1.call-done = f32[2048,128]{1,0:T(8,128)} async-done(((f32[2048,128]{1,0:T(8,128)}), f32[2048,128]{1,0:T(8,128)}) %all-reduce.3.cloned.1.call-update) | async-done | bytes 1048592 | tf_op jit(solution)/shard_map/psum | solution.py:149
  333.0 1.6 fusion.82
  334.6 36.8 %while.75 = (s32[]{:T(128)}, f32[64,256]{1,0:T(8,128)S(1)}, s32[8]{0:T(128)S(1)}, f32[2048,128]{1,0:T(8,128)S(1)}, s32[3,2048]{1,0:T(4,128)}, /*index=5*/f32[3,2...) while((s32[]{:T(128)}, f32[64,256]{1,0:T(8,128)S(1)}, ...), condition=%wide.region_7.10_spmd.clone, body=%wide.region_6.9_spmd.clone.sunk | while | flops 101499656 | bytes 555213 | solution.py:53
  372.8 95.0 %while.77 = (s32[]{:T(128)}, f32[3,256]{0,1:T(8,128)S(1)}, f32[3,384]{0,1:T(8,128)S(1)}, s32[16,256]{1,0:T(8,128)}, f32[64,384]{0,1:T(8,128)S(1)}, /*index=5*/f3...) while((s32[]{:T(128)}, f32[3,256]{0,1:T(8,128)S(1)}, ...), condition=%wide.region_17.20_spmd.clone, body=%wide.region_13.19_spmd.clone.sunk | while | flops 61443 | bytes 443763 | solution.py:138
  375.8 2.5 scatter_custom_fusion.6
  381.7 2.5 scatter_custom_fusion.6
  387.7 2.5 scatter_custom_fusion.6
  393.6 2.5 scatter_custom_fusion.6
  399.6 2.5 scatter_custom_fusion.6
  405.5 2.5 scatter_custom_fusion.6
  411.4 2.5 scatter_custom_fusion.6
  417.4 2.5 scatter_custom_fusion.6
  423.3 2.5 scatter_custom_fusion.6
  429.3 2.5 scatter_custom_fusion.6
  435.2 2.5 scatter_custom_fusion.6
  441.1 2.5 scatter_custom_fusion.6
  447.1 2.5 scatter_custom_fusion.6
  453.0 2.5 scatter_custom_fusion.6
  459.0 2.5 scatter_custom_fusion.6
  464.9 2.5 scatter_custom_fusion.6
  468.8 3.6 collective-permute-start.2
  472.5 49.6 %while.73 = (s32[]{:T(128)}, f32[8,256,128]{2,1,0:T(8,128)S(1)}, s32[8]{0:T(128)S(1)}, s32[3,2048]{1,0:T(4,128)}, f32[3,256]{1,0:T(4,128)S(1)}, /*index=5*/f32[6...) while((s32[]{:T(128)}, f32[8,256,128]{2,1,0:T(8,128)S(1)}, s32[8]{0:T(128)S(1)}, ...), condition=%wide.region_9.12_spmd, body=%wide.region_8.11_spmd.sunk | while | flops 101483264 | bytes 1079775 | solution.py:53
  476.5 1.4 fusion.152
  482.7 1.4 fusion.152
  488.9 1.4 fusion.152
  495.1 1.4 fusion.152
  501.3 1.4 fusion.152
  507.5 1.4 fusion.152
  513.7 1.4 fusion.152
  519.9 1.4 fusion.152
  523.7 1.9 collective-permute-start.3
  525.9 4.2 collective-permute-done.3
  530.9 261.6 %all-reduce.5.cloned.1.call-done = f32[2048,128]{1,0:T(8,128)} async-done(((f32[2048,128]{1,0:T(8,128)}), f32[2048,128]{1,0:T(8,128)}) %all-reduce.5.cloned.1.call-update) | async-done | bytes 1048592 | tf_op jit(solution)/shard_map/psum | solution.py:162
  792.5 1.6 fusion.81
  794.1 37.2 %while.76 = (s32[]{:T(128)}, f32[3,256]{1,0:T(4,128)S(1)}, s32[8]{0:T(128)S(1)}, s32[3,2048]{1,0:T(4,128)}, f32[3,256]{1,0:T(4,128)S(1)}, /*index=5*/f32[2048,12...) while((s32[]{:T(128)}, f32[3,256]{1,0:T(4,128)S(1)}, ...), condition=%wide.region_12.15_spmd.clone, body=%wide.region_11.14_spmd.clone.sunk | while | flops 204737536 | bytes 2137305 | solution.py:53
  (629 shorter events, 227.9 us)
Async XLA Ops:
  7.2 0.8 copy-start.2
  7.2 325.8 %all-reduce.3.cloned.1.call-start = ((), (), s32[]{:S(2)}) async-start(), calls=%async_computation | async-start | bytes 2097152 | tf_op jit(solution)/shard_map/psum | solution.py:149
  8.1 55.4 %collective-permute-start = (f32[67,64]{1,0:T(8,128)S(1)}, f32[67,64]{1,0:T(8,128)S(1)}, u32[]{:S(2)}, u32[]{:S(2)}) collective-permute-start(f32[67,64]{1,0:T(8,128)S(1)} %get-tuple-element.592), channel_id=1, source_target_pairs={{0,32},{32,64},{64,96},{96,128},{128,160},{160,192},{192,224},{224... | collective-permute-start | bytes 51464 | tf_op jit(solution)/shard_map/ppermute | solution.py:24
  12.9 50.6 %collective-permute-start.1 = (f32[67,64]{1,0:T(8,128)S(1)}, f32[67,64]{1,0:T(8,128)S(1)}, u32[]{:S(2)}, u32[]{:S(2)}) collective-permute-start(f32[67,64]{1,0:T(8,128)S(1)} %get-tuple-element.593), channel_id=1, source_target_pairs={{32,0},{64,32},{96,64},{128,96},{160,128},{192,160},{224,192},{256... | collective-permute-start | bytes 51464 | tf_op jit(solution)/shard_map/ppermute | solution.py:25
  61.1 1.0 copy-start.1
  61.1 1.4 copy-start.3
  62.1 730.4 %all-reduce.5.cloned.1.call-start = ((), (), s32[]{:S(2)}) async-start(), calls=%async_computation.1 | async-start | bytes 2097152 | tf_op jit(solution)/shard_map/psum | solution.py:162
  334.6 36.8 %copy-start.4 = (bf16[64,256]{1,0:T(8,128)(2,1)S(1)}, bf16[64,256]{1,0:T(8,128)(2,1)}, u32[]{:S(2)}) copy-start(bf16[64,256]{1,0:T(8,128)(2,1)} %param.27) | copy-start | bytes 98308
  371.4 0.7 copy-start.6
  468.8 56.9 %collective-permute-start.2 = (f32[3,64]{1,0:T(4,128)}, f32[3,64]{1,0:T(4,128)S(1)}, u32[]{:S(2)}, u32[]{:S(2)}) collective-permute-start(f32[3,64]{1,0:T(4,128)} %get-tuple-element.595), channel_id=1, source_target_pairs={{32,0},{64,32},{96,64},{128,96},{160,128},{192,160},{224,192},{256... | collective-permute-start | bytes 2312 | tf_op jit(solution)/shard_map/ppermute | solution.py:25
  472.5 0.6 copy-start.7
  478.0 0.7 copy-start.8
  478.7 0.6 copy-start.7
  484.2 0.7 copy-start.8
  484.9 0.6 copy-start.7
  490.4 0.7 copy-start.8
  491.1 0.6 copy-start.7
  496.6 0.7 copy-start.8
  497.3 0.6 copy-start.7
  502.8 0.7 copy-start.8
  503.5 0.6 copy-start.7
  509.0 0.7 copy-start.8
  509.6 0.6 copy-start.7
  515.2 0.7 copy-start.8
  515.8 0.6 copy-start.7
  521.4 0.7 copy-start.8
  522.0 1.0 copy-start
  523.1 0.7 copy-start.5
  523.7 6.4 collective-permute-start.3
Sparse Core Ops, SparseCore 0:
  62.2 270.7 all-reduce.2
  523.2 269.2 all-reduce.4
where the time goes:
time: 842 us; the launch traced here: 839 us
  waiting for transfers between devices  487 us (58%)
  other arithmetic  112 us (13%)
  local copies, waits for them, and re-layouts  96.6 us (11%)
  matrix products  84.5 us (10%)
  loops' own time  23.9 us (3%)
  starting transfers between devices  19.9 us (2%)
  between operations  14.4 us (2%)
    psum x1, waiting for transfers between devices, on_device(): grads_sum = lax.psum(grad_partial, ('slab', 'sub'))  262 us
    psum x1, waiting for transfers between devices, on_device(): factor = lax.psum(partial_value, ('slab', 'sub'))  221 us
    dot_general x72, matrix products, exact_dot(): jnp.dot(left, right, precision=lax.Precision.HIGHEST, preferred_element_t...  84.5 us
    scatter-add x16, other arithmetic, one_slot(): ext_acc = ext_acc.at[:, index_row].add(-force_term)  39.5 us
    gather x32, local copies, waits for them, and re-layouts, one_slot(): near_feat = jnp.take(ext_feat, index_row, axis=1)  23.6 us
    gather x32, local copies, waits for them, and re-layouts, one_slot(): near_pos = jnp.take(ext_pos, index_row, axis=1)  23.3 us
    another operation x4, loops' own time, over_kvec(): lax.scan(advance, running, jnp.arange(kvec_total // block_size, dtype=jnp...  22.7 us
    dynamic_slice x32, local copies, waits for them, and re-layouts, over_kvec(): lax.scan(advance, running, jnp.arange(kvec_total // block_size, dtype=jnp...  19.4 us
  transfers between devices with their start and end apart: 6, of which 3 were waited for; matrix products, arithmetic and copies ran while one was open for 14% of the time, Pallas kernels for 0%

commit v1 on v0

v1 whole, which is shorter than its diff:
```python
import functools
import math

import jax
import jax.numpy as jnp
import numpy as np
from jax import lax
from jax.experimental import pallas as pl
from jax.experimental.pallas import tpu as pltpu
from jax.sharding import PartitionSpec as P

F32 = jnp.float32
BF16 = jnp.bfloat16
MESH = pl.DeviceIdType.MESH
TWO_PI = 2.0 * math.pi

NZ, NY, NX, NC = 8, 8, 4, 2
ATOMS_DEV = 256
GHOST = 64
NBR = 16
HALF = 41
GROUP = NZ * NC
WIDE = GROUP * ATOMS_DEV
CHUNK = 1024

RING = sorted(
    [(dz, dc) for dz in range(NZ) for dc in range(NC)],
    key=lambda o: (min(o[0], NZ - o[0]), o[0], o[1]),
)
ARRIVALS = ((0, 2), (2, 6), (6, 10), (10, 14), (14, 16))


def cos_coefficients():
    nodes = np.cos(np.pi * (np.arange(64) + 0.5) / 64)
    square = (nodes + 1) / 8
    fit = np.polynomial.chebyshev.Chebyshev.fit(
        square, np.cos(2 * np.pi * np.sqrt(square)), 7, domain=[0, 0.25]
    )
    return [float(v) for v in fit.convert(kind=np.polynomial.Polynomial).coef]


COS = cos_coefficients()


def cos_turns(turns):
    reduced = turns - jnp.round(turns)
    square = reduced * reduced
    value = jnp.full_like(square, COS[-1])
    for factor in COS[-2::-1]:
        value = value * square + factor
    return value


def halves(value):
    high = value.astype(BF16).astype(F32)
    return high, value - high


def stacked_halves(value):
    return jnp.concatenate(halves(value), 0).astype(BF16)


def dot(left, right, contract=(1, 0)):
    return lax.dot_general(
        left, right, (((contract[0],), (contract[1],)), ((), ())), preferred_element_type=F32
    )


def exact(left, right, contract=(1, 0)):
    return lax.dot_general(
        left,
        right,
        (((contract[0],), (contract[1],)), ((), ())),
        precision=lax.Precision.HIGHEST,
        preferred_element_type=F32,
    )


def rows_like(shape):
    return lax.broadcasted_iota(jnp.int32, shape, 0)


def lanes_like(shape):
    return lax.broadcasted_iota(jnp.int32, shape, 1)


def turn_rows(value):
    return pltpu.roll(value, 4, 0)


def turn_lanes(value, by):
    return pltpu.roll(value, by % 128, 1)


def swap_sides(value):
    lane = lanes_like(value.shape)
    return jnp.where(lane < HALF, turn_lanes(value, -HALF), turn_lanes(value, HALF))


def pack_modes(modes):
    lane = lanes_like((8, 128))
    row = rows_like((8, 128))
    t0, t1, t2, t3, t4 = (modes[8 * i : 8 * i + 8] for i in range(5))
    used = lane < 2 * HALF
    return jnp.concatenate(
        [
            jnp.where(used, t0, turn_lanes(t3, 2 * HALF)),
            jnp.where(used, t1, turn_lanes(t3, HALF)),
            jnp.where(
                used, t2, jnp.where(row < 4, turn_lanes(t4, 2 * HALF), turn_lanes(t4, HALF))
            ),
        ],
        0,
    )


def unpack_modes(packed):
    lane = lanes_like((8, 128))
    row = rows_like((8, 128))
    p0, p1, p2 = (packed[8 * i : 8 * i + 8] for i in range(3))
    used = lane < 2 * HALF
    t0, t1, t2 = (jnp.where(used, p, 0.0) for p in (p0, p1, p2))
    t3 = jnp.where(lane < HALF, turn_lanes(p0, -2 * HALF), turn_lanes(p1, -HALF))
    t4 = jnp.where(lane < HALF, turn_lanes(p2, -2 * HALF), turn_lanes(turn_rows(p2), -HALF))
    t3 = jnp.where(used, t3, 0.0)
    t4 = jnp.where(used & (row < 4), t4, 0.0)
    return t0, t1, t2, t3, t4


def weigh(packed, filters):
    t0, t1, t2, t3, t4 = unpack_modes(packed)
    sum12, sum34, sum0 = filters[0:8], filters[8:16], filters[16:24]
    dif12, dif34 = filters[24:32], filters[32:40]
    return jnp.concatenate(
        [
            sum12 * t0 + dif12 * swap_sides(t2),
            sum34 * t1 + dif34 * swap_sides(t3),
            sum12 * t2 - dif12 * swap_sides(t0),
            sum34 * t3 - dif34 * swap_sides(t1),
            sum0 * t4,
        ],
        0,
    )


def with_slopes(weighted):
    lane = lanes_like(weighted.shape)
    pair = jnp.where(lane < HALF, lane, lane - HALF)
    along_y = (pair + 4) // 9
    along_z = pair - 9 * along_y
    sign = jnp.where(lane < HALF, TWO_PI, -TWO_PI)
    sign = jnp.where(lane < 2 * HALF, sign, 0.0)
    swapped = swap_sides(weighted)
    return jnp.concatenate(
        [
            weighted,
            swapped * (sign * along_y.astype(F32)),
            swapped * (sign * along_z.astype(F32)),
        ],
        0,
    )


def left_operand(modes):
    high, low = halves(modes)
    return jnp.concatenate(
        [
            jnp.concatenate([high, high], 1),
            jnp.concatenate([low, jnp.zeros_like(low)], 1),
        ],
        0,
    ).astype(BF16)


def kernel(
    pos_ref,
    feat_ref,
    near_ref,
    miller_ref,
    filter_ref,
    energy_ref,
    upd_ref,
    force_ref,
    tx1,
    rx1,
    ext,
    basis,
    xbasis,
    feat8,
    grad8,
    slopes,
    pairs,
    y1,
    x1,
    y2,
    x2,
    part1,
    part1x,
    part2,
    part2x,
    tx_short,
    rx_short,
    tx_upd,
    rx_upd,
    tx_force,
    rx_force,
    ghost_out,
    ghost_in,
    first_sem,
    recv_sem,
    send_sem,
):
    slab = lax.axis_index("slab")
    sub = lax.axis_index("sub")
    z = lax.rem(slab, NZ)
    x_lo = slab // NZ
    y = sub // 4
    x_hi = lax.rem(sub // 2, 2)
    core = lax.rem(sub, 2)
    x = x_hi * 2 + x_lo

    def at(zz, cc):
        return {"slab": x_lo * NZ + zz, "sub": y * 4 + x_hi * 2 + cc}

    def ring(off):
        return lax.rem(z + off[0], NZ), lax.rem(core + off[1], NC)

    def ring_back(off):
        return lax.rem(z + NZ - off[0], NZ), lax.rem(core + off[1], NC)

    def along_y(d):
        return {"slab": slab, "sub": lax.rem(y + d, NY) * 4 + x_hi * 2 + core}

    def along_x(d):
        xx = lax.rem(x + d, NX)
        return {"slab": lax.rem(xx, 2) * NZ + z, "sub": y * 4 + (xx // 2) * 2 + core}

    upper = {"slab": lax.rem(slab + 1, 16), "sub": sub}
    lower = {"slab": lax.rem(slab + 15, 16), "sub": sub}

    def send(src, dst, send_at, recv, device):
        pltpu.make_async_remote_copy(
            src_ref=src,
            dst_ref=dst,
            send_sem=send_at,
            recv_sem=recv,
            device_id=device,
            device_id_type=MESH,
        ).start()

    def wait(ref, sem):
        pltpu.make_async_copy(ref, ref, sem).wait()

    barrier = pltpu.get_barrier_semaphore()
    greeted = [at(*ring(off)) for off in RING[:0:-1]]
    greeted += [along_y(d) for d in range(1, NY)]
    greeted += [along_x(d) for d in range(1, NX)]
    greeted += [upper, lower]
    for device in greeted:
        pl.semaphore_signal(barrier, inc=1, device_id=device, device_id_type=MESH)

    row8 = rows_like((8, ATOMS_DEV))
    tile_row = rows_like((8, 128))
    first4 = row8 < 4

    feats = feat_ref[...].astype(F32)
    place = jnp.concatenate([pos_ref[...], jnp.zeros((5, ATOMS_DEV), F32)], 0)
    ext[0:64, 128:384] = feats
    ext[64:72, 128:384] = place
    place4 = turn_rows(place)
    for m in range(NZ):
        rows = feats[8 * m : 8 * m + 8]
        tx1[16 * m : 16 * m + 8] = jnp.where(first4, rows, place4)
        tx1[16 * m + 8 : 16 * m + 16] = jnp.where(first4, turn_rows(rows), place4)
    own = z * NC + core
    rx1[:, 0:ATOMS_DEV] = tx1[pl.ds(pl.multiple_of(own * 8, 8), 8)]

    basis[96:128] = jnp.zeros((32, WIDE), BF16)
    basis[224:256] = jnp.zeros((32, WIDE), BF16)

    pl.semaphore_wait(barrier, len(greeted))

    for r in range(GROUP - 1, 0, -1):
        zz, cc = ring(RING[r])
        group = [g for g, (lo, hi) in enumerate(ARRIVALS) if lo <= r < hi][0]
        send(
            tx1.at[pl.ds(pl.multiple_of((zz * NC + cc) * 8, 8), 8)],
            rx1.at[:, pl.ds(r * ATOMS_DEV, ATOMS_DEV)],
            send_sem.at[0],
            first_sem.at[group],
            at(zz, cc),
        )
    send(ext.at[:, pl.ds(256, 128)], ext.at[:, pl.ds(0, 128)], send_sem.at[1], recv_sem.at[1], upper)
    send(ext.at[:, pl.ds(128, 128)], ext.at[:, pl.ds(384, 128)], send_sem.at[1], recv_sem.at[1], lower)

    m0 = miller_ref[0:1, :]
    code = 9 * miller_ref[1:2, :] + miller_ref[2:3, :]
    code = jnp.where(m0 < 0, -code, code)
    first = jnp.abs(m0)
    pair_at = jnp.abs(code)
    sign = jnp.where(code < 0, -1.0, 1.0)
    kvec = miller_ref.shape[1]
    row128 = rows_like((128, kvec))
    side = jnp.where(row128 < HALF, row128, row128 - HALF)
    hit = (side == pair_at) & (row128 < 2 * HALF)
    plain = jnp.where(hit, 1.0, 0.0)
    signed = jnp.where(hit, jnp.where(row128 < HALF, -sign, sign), 0.0)
    table = jnp.concatenate([plain, signed], 0).astype(BF16)
    channel = 8 * z + 4 * core
    pick = jnp.where(
        lanes_like((8, 64)) == channel + lax.rem(rows_like((8, 64)), 4), 1.0, 0.0
    )
    mine = exact(pick, filter_ref[...], (1, 1))
    upper_rows = rows_like((8, kvec)) // 4
    taken = jnp.concatenate(
        [
            jnp.where(first == 1 + upper_rows, mine, 0.0),
            jnp.where(first == 3 + upper_rows, mine, 0.0),
            jnp.where(first == 0, mine, 0.0),
        ],
        0,
    )
    big = taken.astype(BF16).astype(F32)
    left = taken - big
    middle = left.astype(BF16).astype(F32)
    taken = jnp.concatenate([big, middle, left - middle, jnp.zeros((8, kvec), F32)], 0)
    summed = dot(taken.astype(BF16), table, (1, 1))
    summed = summed[0:24] + summed[24:48] + summed[48:72]
    atoms_all = ATOMS_DEV * lax.axis_size("slab") * lax.axis_size("sub")
    scale = 1.0 / math.sqrt(atoms_all * kvec)
    filters = scale * jnp.concatenate([summed[:, 0:128], summed[0:16, 128:256]], 0)

    energy_row = energy_ref[...]
    energy8 = jnp.sum(pick * energy_row, 1, keepdims=True)
    energy64 = jnp.sum(
        jnp.where(rows_like((64, 64)) == lanes_like((64, 64)), energy_row, 0.0),
        1,
        keepdims=True,
    )

    near = near_ref[...]
    ext_row = rows_like((ATOMS_DEV + 2 * GHOST, ATOMS_DEV))
    count = jnp.zeros(ext_row.shape, F32)
    for n in range(NBR):
        count = count + jnp.where(ext_row == near[n : n + 1, :], 1.0, 0.0)
    pairs[0:64] = jnp.zeros((64, ATOMS_DEV), F32)
    pairs[448:512] = jnp.zeros((64, ATOMS_DEV), F32)
    pairs[64:448] = count

    total = jnp.zeros((80, 256), F32)
    for group, (lo, hi) in enumerate(ARRIVALS):
        width = (hi - lo) * ATOMS_DEV
        here = slice(lo * ATOMS_DEV, hi * ATOMS_DEV)
        recv = rx1.at[:, pl.ds(max(lo, 1) * ATOMS_DEV, (hi - max(lo, 1)) * ATOMS_DEV)]
        wait(recv, first_sem.at[group])
        block = rx1[:, here]
        row = rows_like((88, width))
        pair = jnp.where(row < HALF, row, row - HALF)
        by = (pair + 4) // 9
        cz = (pair - 9 * by).astype(F32)
        shift = jnp.where(row < HALF, 0.0, 0.25)
        turns = by.astype(F32) * block[5:6] + cz * block[6:7] - shift
        waves = jnp.where(row < 2 * HALF, cos_turns(turns), 0.0)
        high, low = halves(waves)
        gap = jnp.zeros((8, width), F32)
        basis[0:96, here] = jnp.concatenate([high, gap], 0).astype(BF16)
        basis[128:224, here] = jnp.concatenate([low, gap], 0).astype(BF16)
        order = (1 + rows_like((8, width)) // 4).astype(F32)
        turns12 = order * block[4:5]
        turns34 = (order + 2.0) * block[4:5]
        waves_x = [
            cos_turns(turns12),
            cos_turns(turns34),
            cos_turns(turns12 - 0.25),
            cos_turns(turns34 - 0.25),
        ]
        for i, wave in enumerate(waves_x):
            xbasis[8 * i : 8 * i + 8, here] = wave
        value = jnp.where(rows_like((8, width)) < 4, block, turn_rows(block))
        feat8[:, here] = value
        modes = jnp.concatenate([value * wave for wave in waves_x] + [value], 0)
        total = total + dot(stacked_halves(modes), basis[:, here], (1, 1))
    own_modes = total[0:40, 0:128] + total[0:40, 128:256] + total[40:80, 0:128]

    def add_y(own_part, src, buf, index, later):
        src[...] = own_part
        for d in range(1, NY):
            send(src, buf.at[d - 1], send_sem.at[index], recv_sem.at[index], along_y(d))
        later()
        wait(buf, recv_sem.at[index])
        out = src[...]
        for d in range(NY - 1):
            out = out + buf[d]
        return out

    def add_x(own_part, src, buf, index, later):
        src[...] = own_part
        for d in range(1, NX):
            send(src, buf.at[d - 1], send_sem.at[index], recv_sem.at[index], along_x(d))
        later()
        wait(buf, recv_sem.at[index])
        out = src[...]
        for d in range(NX - 1):
            out = out + buf[d]
        return out

    def trig_rows(position):
        valid = rows_like(position.shape) < 3
        return jnp.concatenate(
            [
                jnp.where(valid, cos_turns(position), 0.0),
                jnp.where(valid, cos_turns(position - 0.25), 0.0),
            ],
            0,
        )

    def short_values():
        wait(ext.at[:, pl.ds(0, 256)], recv_sem.at[1])
        trig = trig_rows(ext[64:72])
        high, low = halves(trig)
        left_side = jnp.concatenate([high, low, high], 0).astype(BF16)
        right_side = jnp.concatenate([high, high, low], 0)[:, 128:384].astype(BF16)
        closeness = dot(left_side, right_side, (0, 0))
        weights = pairs[...] * jnp.exp(closeness - 3.0)
        pairs[...] = weights
        high, low = halves(weights)
        ext_feat = ext[0:64].astype(BF16)
        short = 0.25 * (dot(ext_feat, high.astype(BF16)) + dot(ext_feat, low.astype(BF16)))
        for m in range(NZ):
            rows = short[8 * m : 8 * m + 8]
            turned = turn_rows(rows)
            tx_short[2 * m] = jnp.where(tile_row < 4, rows[:, 0:128], turned[:, 128:256])
            tx_short[2 * m + 1] = jnp.where(tile_row < 4, turned[:, 0:128], rows[:, 128:256])
        rx_short[0] = tx_short[own]
        for r in range(GROUP - 1, 0, -1):
            zz, cc = ring(RING[r])
            send(
                tx_short.at[zz * NC + cc], rx_short.at[r], send_sem.at[2], recv_sem.at[2], at(zz, cc)
            )

    part = add_y(pack_modes(own_modes), part1, y1, 3, short_values)
    factor = add_x(part, part1x, x1, 4, lambda: None)
    weighted = weigh(factor, filters)
    operand = left_operand(weighted)
    wait(rx_short.at[pl.ds(1, GROUP - 1)], recv_sem.at[2])

    total = jnp.zeros((80, 256), F32)
    blocks = CHUNK // ATOMS_DEV
    for chunk in range(WIDE // CHUNK):
        here = slice(chunk * CHUNK, (chunk + 1) * CHUNK)
        waves_x = [xbasis[8 * i : 8 * i + 8, here] for i in range(4)]
        found = dot(operand, basis[:, here])
        found = found[0:40] + found[40:80]
        field = found[32:40]
        for i in range(4):
            field = field + found[8 * i : 8 * i + 8] * waves_x[i]
        field = field + turn_rows(field)
        pieces = []
        for b in range(blocks):
            tile = rx_short[chunk * blocks + b]
            turned = turn_rows(tile)
            pieces += [
                jnp.where(tile_row < 4, tile, turned),
                jnp.where(tile_row < 4, turned, tile),
            ]
        updated = feat8[:, here] + jnp.concatenate(pieces, 1) + field
        for b in range(blocks):
            tx_upd[chunk * blocks + b] = jnp.where(
                tile_row < 4,
                updated[:, b * 256 : b * 256 + 128],
                updated[:, b * 256 + 128 : b * 256 + 256],
            )
        squashed = jnp.tanh(updated)
        gradient = energy8 * (1.0 - squashed * squashed)
        grad8[:, here] = gradient
        modes = jnp.concatenate([gradient * wave for wave in waves_x] + [gradient], 0)
        total = total + dot(stacked_halves(modes), basis[:, here], (1, 1))
    own_modes = total[0:40, 0:128] + total[0:40, 128:256] + total[40:80, 0:128]

    order12 = (TWO_PI * (1 + rows_like((8, CHUNK)) // 4)).astype(F32)
    order34 = order12 + 2.0 * TWO_PI

    def field_slopes(slope_operand, here):
        c12, c34, s12, s34 = (xbasis[8 * i : 8 * i + 8, here] for i in range(4))
        found = dot(slope_operand, basis[:, here])
        found = found[0:120] + found[120:240]
        t = [found[8 * i : 8 * i + 8] for i in range(15)]
        along = [order12 * (c12 * t[2] - s12 * t[0]) + order34 * (c34 * t[3] - s34 * t[1])]
        for base in (5, 10):
            along.append(
                t[base + 4]
                + c12 * t[base]
                + c34 * t[base + 1]
                + s12 * t[base + 2]
                + s34 * t[base + 3]
            )
        return along

    def first_slopes():
        rx_upd[own] = tx_upd[0]
        for r in range(GROUP - 1, 0, -1):
            zz, cc = ring_back(RING[r])
            send(tx_upd.at[r], rx_upd.at[own], send_sem.at[5], recv_sem.at[5], at(zz, cc))
        slope_operand = left_operand(with_slopes(weighted))
        for chunk in range(WIDE // CHUNK):
            here = slice(chunk * CHUNK, (chunk + 1) * CHUNK)
            gradient = grad8[:, here]
            for d, value in enumerate(field_slopes(slope_operand, here)):
                slopes[8 * d : 8 * d + 8, here] = gradient * value

    short_force = []

    def short_forces():
        others = rx_upd.at[pl.ds(0, GROUP - 1)]
        wait(others, recv_sem.at[5])
        for m in range(NZ):
            low, high = rx_upd[2 * m], rx_upd[2 * m + 1]
            upd_ref[8 * m : 8 * m + 8, 0:128] = jnp.where(tile_row < 4, low, turn_rows(high))
            upd_ref[8 * m : 8 * m + 8, 128:256] = jnp.where(tile_row < 4, turn_rows(low), high)
        squashed = jnp.tanh(upd_ref[...])
        gradient = energy64 * (1.0 - squashed * squashed)
        ext_feat = ext[0:64]
        doubled = jnp.concatenate([ext_feat, ext_feat], 0).astype(BF16)
        touch = dot(doubled, stacked_halves(gradient), (0, 0))
        force = (-0.25 * TWO_PI) * touch * pairs[...]
        high, low = halves(force)
        high, low = high.astype(BF16), low.astype(BF16)
        trig = trig_rows(ext[64:72])
        trig_own = trig[:, 128:384]
        both = stacked_halves(trig)
        found_h, found_l = dot(both, high), dot(both, low)
        found = found_h[0:16] + found_h[16:32] + found_l[0:16]
        mine_acc = trig_own[8:16] * found[0:8] - trig_own[0:8] * found[8:16]
        both = stacked_halves(trig_own)
        found_h, found_l = dot(both, high, (1, 1)), dot(both, low, (1, 1))
        found = found_h[0:16] + found_h[16:32] + found_l[0:16]
        ext_acc = trig[8:16] * found[0:8] - trig[0:8] * found[8:16]
        ghost_out[0] = ext_acc[:, 0:128]
        ghost_out[1] = ext_acc[:, 384:512]
        send(ghost_out.at[0], ghost_in.at[1], send_sem.at[6], recv_sem.at[6], lower)
        send(ghost_out.at[1], ghost_in.at[0], send_sem.at[6], recv_sem.at[6], upper)
        short_force.append(mine_acc + ext_acc[:, 128:384])

    part = add_y(pack_modes(own_modes), part2, y2, 7, first_slopes)
    factor = add_x(part, part2x, x2, 8, short_forces)
    slope_operand = left_operand(with_slopes(weigh(factor, filters)))
    for chunk in range(WIDE // CHUNK):
        here = slice(chunk * CHUNK, (chunk + 1) * CHUNK)
        value = feat8[:, here]
        sums = [
            jnp.sum(slopes[8 * d : 8 * d + 8, here] + value * along, 0, keepdims=True)
            for d, along in enumerate(field_slopes(slope_operand, here))
        ]
        sums = jnp.concatenate(sums + [jnp.zeros((5, CHUNK), F32)], 0)
        for b in range(blocks):
            tx_force[chunk * blocks + b] = jnp.where(
                tile_row < 4,
                sums[:, b * 256 : b * 256 + 128],
                turn_rows(sums[:, b * 256 + 128 : b * 256 + 256]),
            )
    for r in range(GROUP - 1, 0, -1):
        send(
            tx_force.at[r],
            rx_force.at[r - 1],
            send_sem.at[9],
            recv_sem.at[9],
            at(*ring_back(RING[r])),
        )
    wait(ghost_in, recv_sem.at[6])
    rest = short_force[0] + jnp.concatenate([ghost_in[0], ghost_in[1]], 1)
    wait(rx_force, recv_sem.at[9])
    pulled = tx_force[0]
    for r in range(GROUP - 1):
        pulled = pulled + rx_force[r]
    rest = rest + jnp.concatenate([pulled, turn_rows(pulled)], 1)
    force_ref[...] = -rest[0:3]

    wait(tx1.at[pl.ds(0, 8 * (GROUP - 1))], send_sem.at[0])
    wait(ext.at[:, pl.ds(0, 256)], send_sem.at[1])
    wait(tx_short.at[pl.ds(0, GROUP - 1)], send_sem.at[2])
    wait(y1, send_sem.at[3])
    wait(x1, send_sem.at[4])
    wait(tx_upd.at[pl.ds(0, GROUP - 1)], send_sem.at[5])
    wait(ghost_out, send_sem.at[6])
    wait(y2, send_sem.at[7])
    wait(x2, send_sem.at[8])
    wait(tx_force.at[pl.ds(0, GROUP - 1)], send_sem.at[9])


def on_device(positions, features, neighbours, miller, filter_weights, energy_weights):
    vmem = pl.BlockSpec(memory_space=pltpu.VMEM)
    scratch = [
        ((GROUP * 8, ATOMS_DEV), F32),
        ((8, WIDE), F32),
        ((72, 512), F32),
        ((256, WIDE), BF16),
        ((32, WIDE), F32),
        ((8, WIDE), F32),
        ((8, WIDE), F32),
        ((24, WIDE), F32),
        ((512, ATOMS_DEV), F32),
        ((NY - 1, 24, 128), F32),
        ((NX - 1, 24, 128), F32),
        ((NY - 1, 24, 128), F32),
        ((NX - 1, 24, 128), F32),
        ((24, 128), F32),
        ((24, 128), F32),
        ((24, 128), F32),
        ((24, 128), F32),
        ((GROUP, 8, 128), F32),
        ((GROUP, 8, 128), F32),
        ((GROUP, 8, 128), F32),
        ((GROUP, 8, 128), F32),
        ((GROUP, 8, 128), F32),
        ((GROUP - 1, 8, 128), F32),
        ((2, 8, 128), F32),
        ((2, 8, 128), F32),
    ]
    return pl.pallas_call(
        kernel,
        out_shape=(
            jax.ShapeDtypeStruct((64, ATOMS_DEV), F32),
            jax.ShapeDtypeStruct((3, ATOMS_DEV), F32),
        ),
        in_specs=[vmem] * 6,
        out_specs=(vmem, vmem),
        scratch_shapes=[pltpu.VMEM(shape, kind) for shape, kind in scratch]
        + [
            pltpu.SemaphoreType.DMA((len(ARRIVALS),)),
            pltpu.SemaphoreType.DMA((10,)),
            pltpu.SemaphoreType.DMA((10,)),
        ],
        compiler_params=pltpu.CompilerParams(
            collective_id=0, has_side_effects=True, vmem_limit_bytes=40 * 2**20
        ),
    )(positions, features, neighbours, miller, filter_weights, energy_weights.reshape(1, 64))


def solution(mesh):
    split = P(None, ("slab", "sub"))
    return jax.shard_map(
        on_device,
        mesh=mesh,
        in_specs=(split, split, split, P(), P(), P()),
        out_specs=(split, split),
        check_vma=False,
    )
```

time: 842 us -> 50.4 us (0.06)
  waiting for transfers between devices: 487 us -> 0 us
  other arithmetic: 112 us -> 0 us
  local copies, waits for them, and re-layouts: 96.6 us -> 2.64 us
  matrix products: 84.5 us -> 0 us
  Pallas kernels: 0 us -> 46.9 us
  loops' own time: 23.9 us -> 0 us
  starting transfers between devices: 19.9 us -> 0 us
  between operations: 14.4 us -> 0.73 us
    psum x2 -> x0, waiting for transfers between devices: 483 us -> none  [the longest x1 262 us: on_device(): grads_sum = lax.psum(grad_partial, ('slab', 'sub'))]
    dot_general x72 -> x0, matrix products: 84.5 us -> none  [exact_dot(): jnp.dot(left, right, precision=lax.Precision.HIGHEST, preferred_element_t...]
    gather x64 -> x0, local copies, waits for them, and re-layouts: 46.9 us -> none  [the longest x32 23.6 us: one_slot(): near_feat = jnp.take(ext_feat, index_row, axis=1)]
    pallas_call x0 -> x1, Pallas kernels: none -> 46.9 us  [on_device(): pl.pallas_call(kernel, out_shape=(jax.ShapeDtypeStruct((64, ATOMS_DEV), F...]
    scatter-add x16 -> x0, other arithmetic: 39.5 us -> none  [one_slot(): ext_acc = ext_acc.at[:, index_row].add(-force_term)]
    dynamic_slice x48 -> x0, local copies, waits for them, and re-layouts: 30.7 us -> none  [the longest x32 19.4 us: over_kvec(): lax.scan(advance, running, jnp.arange(kvec_total // block_size, dtype=jnp...]
    another operation x6 -> x0, loops' own time: 23.9 us -> none  [the longest x4 22.7 us: over_kvec(): lax.scan(advance, running, jnp.arange(kvec_total // block_size, dtype=jnp...]
    convert_element_type x33 -> x0, other arithmetic: 23 us -> none  [the longest x24 16.6 us: phase_pair(): miller_float = miller_block.astype(jnp.float32)]
  transfers between devices with their start and end apart: 6 -> 0, of which waited for: 3 -> 0; matrix products, arithmetic and copies ran while one was open for 14% -> 0% of each run, Pallas kernels for 0% -> 0%
where the time goes in v1:
time: 50.4 us; the launch traced here: 50.2 us
  Pallas kernels  46.9 us (93%)
  local copies, waits for them, and re-layouts  2.64 us (5%)
  between operations  0.73 us (1%)
    pallas_call x1, Pallas kernels, on_device(): pl.pallas_call(kernel, out_shape=(jax.ShapeDtypeStruct((64, ATOMS_DEV), F...  46.9 us
    unnamed x13, local copies, waits for them, and re-layouts  2.64 us

profile of v1, /device:TPU:1, one launch (start us, length us, event | category | flops | bytes accessed | tf_op | source)
XLA Modules:
  0.0 50.2 jit_solution(3353626529017115066)
XLA Ops:
  0.6 0.0 copy-start
  0.6 0.0 copy-start.1
  0.7 0.0 copy-start.2
  0.7 0.0 copy-start.3
  0.7 0.0 copy-start.4
  0.7 1.4 %copy.8.filter_ref = f32[2048,64]{1,0:T(8,128)S(1)} copy(f32[2048,64]{0,1:T(8,128)} %param.10) | data formatting | bytes 1048576 | tf_op args[4]
  2.1 0.0 copy-done
  2.1 0.0 copy-done.1
  2.1 0.0 copy-done.2
  2.1 0.0 copy-done.3
  2.1 0.0 copy-done.4
  2.1 46.9 %shard_map.77 = (f32[64,256]{1,0:T(8,128)S(1)}, f32[3,256]{1,0:T(4,128)S(1)}) custom-call(f32[3,256]{1,0:T(4,128)S(1)} %copy-done.3, bf16[64,256]{1,0:T(8,128)(2,1)S(1)} %copy-done, s32[16,256]{1,0:T(8,128)S(1)} %copy-done.2, s32[3,2048]{1,0:T(4,128)S(1)} %copy-done.1, f32[2048,64]{1,0:T(8,128)S(1)} %copy.8.filter_ref, f32[1,64]{1,0:T(1,128)S(1)} %bitcast.1), custom_call_target="tpu_custom_call" | custom-call | tf_op jit(solution)/shard_map/pallas_call | solution.py:619
  49.0 0.6 %copy.11 = f32[64,256]{1,0:T(8,128)} copy(f32[64,256]{1,0:T(8,128)S(1)} %get-tuple-element.4) | data formatting | bytes 131072
  49.6 0.6 %copy.12 = f32[3,256]{1,0:T(4,128)} copy(f32[3,256]{1,0:T(4,128)S(1)} %get-tuple-element.5) | data formatting | bytes 6144
Async XLA Ops:
  0.6 1.5 %copy-start = (bf16[64,256]{1,0:T(8,128)(2,1)S(1)}, bf16[64,256]{1,0:T(8,128)(2,1)}, u32[]{:S(2)}) copy-start(bf16[64,256]{1,0:T(8,128)(2,1)} %feat_ref.1) | copy-start | bytes 98308
  0.6 1.5 %copy-start.1 = (s32[3,2048]{1,0:T(4,128)S(1)}, s32[3,2048]{1,0:T(4,128)}, u32[]{:S(2)}) copy-start(s32[3,2048]{1,0:T(4,128)} %miller_ref.1) | copy-start | bytes 73732
  0.7 1.5 %copy-start.2 = (s32[16,256]{1,0:T(8,128)S(1)}, s32[16,256]{1,0:T(8,128)}, u32[]{:S(2)}) copy-start(s32[16,256]{1,0:T(8,128)} %near_ref.1) | copy-start | bytes 49156
  0.7 1.5 %copy-start.3 = (f32[3,256]{1,0:T(4,128)S(1)}, f32[3,256]{1,0:T(4,128)}, u32[]{:S(2)}) copy-start(f32[3,256]{1,0:T(4,128)} %pos_ref.1) | copy-start | bytes 9220
  0.7 1.5 %copy-start.4 = (f32[64]{0:T(128)S(1)}, f32[64]{0:T(128)}, u32[]{:S(2)}) copy-start(f32[64]{0:T(128)} %param.11) | copy-start | bytes 772

commit v2 on v1

--- a/solution.py
+++ b/solution.py
@@ -18,7 +18,8 @@
 ATOMS_DEV = 256
 GHOST = 64
 NBR = 16
-HALF = 41
+HALF = 40
+USED = 2 * HALF + 1
 GROUP = NZ * NC
 WIDE = GROUP * ATOMS_DEV
 CHUNK = 1024
@@ -27,28 +28,31 @@
     [(dz, dc) for dz in range(NZ) for dc in range(NC)],
     key=lambda o: (min(o[0], NZ - o[0]), o[0], o[1]),
 )
+FAR_Y = (4, 3, 5, 2, 6, 1, 7)
+FAR_X = (2, 1, 3)
 ARRIVALS = ((0, 2), (2, 6), (6, 10), (10, 14), (14, 16))
 
 
-def cos_coefficients():
+def wave_coefficients():
     nodes = np.cos(np.pi * (np.arange(64) + 0.5) / 64)
-    square = (nodes + 1) / 8
+    square = (nodes + 1) / 32
+    angle = np.sqrt(square)
     fit = np.polynomial.chebyshev.Chebyshev.fit(
-        square, np.cos(2 * np.pi * np.sqrt(square)), 7, domain=[0, 0.25]
+        square, -np.sin(2 * np.pi * angle) / angle, 5, domain=[0, 1 / 16]
     )
     return [float(v) for v in fit.convert(kind=np.polynomial.Polynomial).coef]
 
 
-COS = cos_coefficients()
+WAVE = wave_coefficients()
 
 
 def cos_turns(turns):
-    reduced = turns - jnp.round(turns)
-    square = reduced * reduced
-    value = jnp.full_like(square, COS[-1])
-    for factor in COS[-2::-1]:
+    beyond = jnp.abs(turns - jnp.round(turns)) - 0.25
+    square = beyond * beyond
+    value = jnp.full_like(square, WAVE[-1])
+    for factor in WAVE[-2::-1]:
         value = value * square + factor
-    return value
+    return value * beyond
 
 
 def halves(value):
@@ -101,14 +105,13 @@
     lane = lanes_like((8, 128))
     row = rows_like((8, 128))
     t0, t1, t2, t3, t4 = (modes[8 * i : 8 * i + 8] for i in range(5))
-    used = lane < 2 * HALF
+    used = lane < USED
+    rest = USED - HALF
     return jnp.concatenate(
         [
-            jnp.where(used, t0, turn_lanes(t3, 2 * HALF)),
-            jnp.where(used, t1, turn_lanes(t3, HALF)),
-            jnp.where(
-                used, t2, jnp.where(row < 4, turn_lanes(t4, 2 * HALF), turn_lanes(t4, HALF))
-            ),
+            jnp.where(used, t0, turn_lanes(t3, USED)),
+            jnp.where(used, t1, turn_lanes(t3, rest)),
+            jnp.where(used, t2, jnp.where(row < 4, turn_lanes(t4, USED), turn_lanes(t4, rest))),
         ],
         0,
     )
@@ -118,13 +121,30 @@
     lane = lanes_like((8, 128))
     row = rows_like((8, 128))
     p0, p1, p2 = (packed[8 * i : 8 * i + 8] for i in range(3))
-    used = lane < 2 * HALF
+    used = lane < USED
+    rest = USED - HALF
     t0, t1, t2 = (jnp.where(used, p, 0.0) for p in (p0, p1, p2))
-    t3 = jnp.where(lane < HALF, turn_lanes(p0, -2 * HALF), turn_lanes(p1, -HALF))
-    t4 = jnp.where(lane < HALF, turn_lanes(p2, -2 * HALF), turn_lanes(turn_rows(p2), -HALF))
+    t3 = jnp.where(lane < HALF, turn_lanes(p0, -USED), turn_lanes(p1, -rest))
+    t4 = jnp.where(lane < HALF, turn_lanes(p2, -USED), turn_lanes(turn_rows(p2), -rest))
     t3 = jnp.where(used, t3, 0.0)
     t4 = jnp.where(used & (row < 4), t4, 0.0)
     return t0, t1, t2, t3, t4
+
+
+def pair_of(lane):
+    last = lane >= HALF - 8
+    inside = lane % 8
+    b = jnp.where(last, jnp.where(inside < 4, inside + 1, 0), lane // 8 + 1)
+    c = jnp.where(last, jnp.where(inside < 4, 4, inside - 3), inside - 4)
+    return b, c
+
+
+def lane_of(code):
+    b = sum((code >= 9 * i - 4).astype(jnp.int32) for i in range(1, 5))
+    c = code - 9 * b
+    inner = jnp.where(c == 4, HALF - 9 + b, 8 * b - 4 + c)
+    lane = jnp.where(b == 0, HALF - 5 + code, inner)
+    return jnp.where(code == 0, 2 * HALF, lane)
 
 
 def weigh(packed, filters):
@@ -145,9 +165,7 @@
 
 def with_slopes(weighted):
     lane = lanes_like(weighted.shape)
-    pair = jnp.where(lane < HALF, lane, lane - HALF)
-    along_y = (pair + 4) // 9
-    along_z = pair - 9 * along_y
+    along_y, along_z = pair_of(jnp.where(lane < HALF, lane, lane - HALF))
     sign = jnp.where(lane < HALF, TWO_PI, -TWO_PI)
     sign = jnp.where(lane < 2 * HALF, sign, 0.0)
     swapped = swap_sides(weighted)
@@ -173,14 +191,20 @@
 
 
 def kernel(
+    pos_hbm,
+    feat_hbm,
+    near_hbm,
+    miller_hbm,
+    filter_hbm,
+    energy_hbm,
+    upd_ref,
+    force_ref,
     pos_ref,
     feat_ref,
     near_ref,
     miller_ref,
     filter_ref,
     energy_ref,
-    upd_ref,
-    force_ref,
     tx1,
     rx1,
     ext,
@@ -209,6 +233,7 @@
     first_sem,
     recv_sem,
     send_sem,
+    load_sem,
 ):
     slab = lax.axis_index("slab")
     sub = lax.axis_index("sub")
@@ -251,18 +276,41 @@
     def wait(ref, sem):
         pltpu.make_async_copy(ref, ref, sem).wait()
 
+    loads = [
+        pltpu.make_async_copy(src, dst, load_sem.at[i])
+        for i, (src, dst) in enumerate(
+            [
+                (pos_hbm, pos_ref),
+                (feat_hbm, feat_ref),
+                (miller_hbm, miller_ref),
+                (filter_hbm, filter_ref),
+                (energy_hbm, energy_ref),
+                (near_hbm, near_ref),
+            ]
+        )
+    ]
+    for load in loads[:2]:
+        load.start()
+
     barrier = pltpu.get_barrier_semaphore()
     greeted = [at(*ring(off)) for off in RING[:0:-1]]
-    greeted += [along_y(d) for d in range(1, NY)]
-    greeted += [along_x(d) for d in range(1, NX)]
+    greeted += [along_y(d) for d in FAR_Y]
+    greeted += [along_x(d) for d in FAR_X]
     greeted += [upper, lower]
     for device in greeted:
         pl.semaphore_signal(barrier, inc=1, device_id=device, device_id_type=MESH)
 
+    for load in loads[2:]:
+        load.start()
+    basis[96:128] = jnp.zeros((32, WIDE), BF16)
+    basis[224:256] = jnp.zeros((32, WIDE), BF16)
+
     row8 = rows_like((8, ATOMS_DEV))
     tile_row = rows_like((8, 128))
     first4 = row8 < 4
 
+    for load in loads[:2]:
+        load.wait()
     feats = feat_ref[...].astype(F32)
     place = jnp.concatenate([pos_ref[...], jnp.zeros((5, ATOMS_DEV), F32)], 0)
     ext[0:64, 128:384] = feats
@@ -274,9 +322,6 @@
         tx1[16 * m + 8 : 16 * m + 16] = jnp.where(first4, turn_rows(rows), place4)
     own = z * NC + core
     rx1[:, 0:ATOMS_DEV] = tx1[pl.ds(pl.multiple_of(own * 8, 8), 8)]
-
-    basis[96:128] = jnp.zeros((32, WIDE), BF16)
-    basis[224:256] = jnp.zeros((32, WIDE), BF16)
 
     pl.semaphore_wait(barrier, len(greeted))
 
@@ -293,43 +338,12 @@
     send(ext.at[:, pl.ds(256, 128)], ext.at[:, pl.ds(0, 128)], send_sem.at[1], recv_sem.at[1], upper)
     send(ext.at[:, pl.ds(128, 128)], ext.at[:, pl.ds(384, 128)], send_sem.at[1], recv_sem.at[1], lower)
 
-    m0 = miller_ref[0:1, :]
-    code = 9 * miller_ref[1:2, :] + miller_ref[2:3, :]
-    code = jnp.where(m0 < 0, -code, code)
-    first = jnp.abs(m0)
-    pair_at = jnp.abs(code)
-    sign = jnp.where(code < 0, -1.0, 1.0)
-    kvec = miller_ref.shape[1]
-    row128 = rows_like((128, kvec))
-    side = jnp.where(row128 < HALF, row128, row128 - HALF)
-    hit = (side == pair_at) & (row128 < 2 * HALF)
-    plain = jnp.where(hit, 1.0, 0.0)
-    signed = jnp.where(hit, jnp.where(row128 < HALF, -sign, sign), 0.0)
-    table = jnp.concatenate([plain, signed], 0).astype(BF16)
+    for load in loads[2:]:
+        load.wait()
     channel = 8 * z + 4 * core
     pick = jnp.where(
         lanes_like((8, 64)) == channel + lax.rem(rows_like((8, 64)), 4), 1.0, 0.0
     )
-    mine = exact(pick, filter_ref[...], (1, 1))
-    upper_rows = rows_like((8, kvec)) // 4
-    taken = jnp.concatenate(
-        [
-            jnp.where(first == 1 + upper_rows, mine, 0.0),
-            jnp.where(first == 3 + upper_rows, mine, 0.0),
-            jnp.where(first == 0, mine, 0.0),
-        ],
-        0,
-    )
-    big = taken.astype(BF16).astype(F32)
-    left = taken - big
-    middle = left.astype(BF16).astype(F32)
-    taken = jnp.concatenate([big, middle, left - middle, jnp.zeros((8, kvec), F32)], 0)
-    summed = dot(taken.astype(BF16), table, (1, 1))
-    summed = summed[0:24] + summed[24:48] + summed[48:72]
-    atoms_all = ATOMS_DEV * lax.axis_size("slab") * lax.axis_size("sub")
-    scale = 1.0 / math.sqrt(atoms_all * kvec)
-    filters = scale * jnp.concatenate([summed[:, 0:128], summed[0:16, 128:256]], 0)
-
     energy_row = energy_ref[...]
     energy8 = jnp.sum(pick * energy_row, 1, keepdims=True)
     energy64 = jnp.sum(
@@ -354,29 +368,40 @@
         recv = rx1.at[:, pl.ds(max(lo, 1) * ATOMS_DEV, (hi - max(lo, 1)) * ATOMS_DEV)]
         wait(recv, first_sem.at[group])
         block = rx1[:, here]
-        row = rows_like((88, width))
-        pair = jnp.where(row < HALF, row, row - HALF)
-        by = (pair + 4) // 9
-        cz = (pair - 9 * by).astype(F32)
-        shift = jnp.where(row < HALF, 0.0, 0.25)
-        turns = by.astype(F32) * block[5:6] + cz * block[6:7] - shift
-        waves = jnp.where(row < 2 * HALF, cos_turns(turns), 0.0)
-        high, low = halves(waves)
+        row = rows_like((8, width))
+        upper_half = row < 4
+        place_x, place_y, place_z = (block[i : i + 1] for i in (4, 5, 6))
+        quad = (row % 4 + 1).astype(F32)
+        turns = quad * jnp.where(upper_half, place_y, place_z)
+        cos_yz, sin_yz = cos_turns(turns), cos_turns(turns - 0.25)
+        turns = (row - 4).astype(F32) * place_z
+        cos_z, sin_z = cos_turns(turns), cos_turns(turns - 0.25)
+        cos_tiles, sin_tiles = [], []
+        for b in range(4):
+            cos_y, sin_y = cos_yz[b : b + 1], sin_yz[b : b + 1]
+            cos_tiles.append(cos_y * cos_z - sin_y * sin_z)
+            sin_tiles.append(sin_y * cos_z + cos_y * sin_z)
+        cos_4z = jnp.where(upper_half, cos_yz[7:8], 1.0)
+        sin_4z = jnp.where(upper_half, sin_yz[7:8], 0.0)
+        cos_tiles.append(cos_yz * cos_4z - sin_yz * sin_4z)
+        sin_tiles.append(sin_yz * cos_4z + cos_yz * sin_4z)
+        one = jnp.where(row == 0, 1.0, 0.0)
+        high, low = halves(jnp.concatenate(cos_tiles + sin_tiles + [one], 0))
         gap = jnp.zeros((8, width), F32)
         basis[0:96, here] = jnp.concatenate([high, gap], 0).astype(BF16)
         basis[128:224, here] = jnp.concatenate([low, gap], 0).astype(BF16)
-        order = (1 + rows_like((8, width)) // 4).astype(F32)
-        turns12 = order * block[4:5]
-        turns34 = (order + 2.0) * block[4:5]
+        turns = (1 + row // 4).astype(F32) * place_x
+        cos_12, sin_12 = cos_turns(turns), cos_turns(turns - 0.25)
+        cos_2, sin_2 = cos_12[4:5], sin_12[4:5]
         waves_x = [
-            cos_turns(turns12),
-            cos_turns(turns34),
-            cos_turns(turns12 - 0.25),
-            cos_turns(turns34 - 0.25),
+            cos_12,
+            cos_12 * cos_2 - sin_12 * sin_2,
+            sin_12,
+            sin_12 * cos_2 + cos_12 * sin_2,
         ]
         for i, wave in enumerate(waves_x):
             xbasis[8 * i : 8 * i + 8, here] = wave
-        value = jnp.where(rows_like((8, width)) < 4, block, turn_rows(block))
+        value = jnp.where(upper_half, block, turn_rows(block))
         feat8[:, here] = value
         modes = jnp.concatenate([value * wave for wave in waves_x] + [value], 0)
         total = total + dot(stacked_halves(modes), basis[:, here], (1, 1))
@@ -384,7 +409,7 @@
 
     def add_y(own_part, src, buf, index, later):
         src[...] = own_part
-        for d in range(1, NY):
+        for d in FAR_Y:
             send(src, buf.at[d - 1], send_sem.at[index], recv_sem.at[index], along_y(d))
         later()
         wait(buf, recv_sem.at[index])
@@ -395,7 +420,7 @@
 
     def add_x(own_part, src, buf, index, later):
         src[...] = own_part
-        for d in range(1, NX):
+        for d in FAR_X:
             send(src, buf.at[d - 1], send_sem.at[index], recv_sem.at[index], along_x(d))
         later()
         wait(buf, recv_sem.at[index])
@@ -438,8 +463,47 @@
                 tx_short.at[zz * NC + cc], rx_short.at[r], send_sem.at[2], recv_sem.at[2], at(zz, cc)
             )
 
+    held_filters = []
+
+    def add_filters():
+        m0 = miller_ref[0:1, :]
+        code = 9 * miller_ref[1:2, :] + miller_ref[2:3, :]
+        code = jnp.where(m0 < 0, -code, code)
+        first = jnp.abs(m0)
+        pair_at = lane_of(jnp.abs(code))
+        sign = jnp.where(code < 0, -1.0, 1.0)
+        kvec = miller_ref.shape[1]
+        row128 = rows_like((128, kvec))
+        side = jnp.where((row128 >= HALF) & (row128 < 2 * HALF), row128 - HALF, row128)
+        hit = side == pair_at
+        plain = jnp.where(hit, 1.0, 0.0)
+        signed = jnp.where(hit & (row128 < 2 * HALF), jnp.where(row128 < HALF, -sign, sign), 0.0)
+        table = jnp.concatenate([plain, signed], 0).astype(BF16)
+        mine = exact(pick, filter_ref[...])
+        upper_rows = rows_like((8, kvec)) // 4
+        taken = jnp.concatenate(
+            [
+                jnp.where(first == 1 + upper_rows, mine, 0.0),
+                jnp.where(first == 3 + upper_rows, mine, 0.0),
+                jnp.where(first == 0, mine, 0.0),
+            ],
+            0,
+        )
+        big = taken.astype(BF16).astype(F32)
+        left = taken - big
+        middle = left.astype(BF16).astype(F32)
+        taken = jnp.concatenate([big, middle, left - middle, jnp.zeros((8, kvec), F32)], 0)
+        summed = dot(taken.astype(BF16), table, (1, 1))
+        summed = summed[0:24] + summed[24:48] + summed[48:72]
+        atoms_all = ATOMS_DEV * lax.axis_size("slab") * lax.axis_size("sub")
+        scale = 1.0 / math.sqrt(atoms_all * kvec)
+        held_filters.append(
+            scale * jnp.concatenate([summed[:, 0:128], summed[0:16, 128:256]], 0)
+        )
+
     part = add_y(pack_modes(own_modes), part1, y1, 3, short_values)
-    factor = add_x(part, part1x, x1, 4, lambda: None)
+    factor = add_x(part, part1x, x1, 4, add_filters)
+    filters = held_filters[0]
     weighted = weigh(factor, filters)
     operand = left_operand(weighted)
     wait(rx_short.at[pl.ds(1, GROUP - 1)], recv_sem.at[2])
@@ -544,7 +608,7 @@
     part = add_y(pack_modes(own_modes), part2, y2, 7, first_slopes)
     factor = add_x(part, part2x, x2, 8, short_forces)
     slope_operand = left_operand(with_slopes(weigh(factor, filters)))
-    for chunk in range(WIDE // CHUNK):
+    for chunk in range(WIDE // CHUNK - 1, -1, -1):
         here = slice(chunk * CHUNK, (chunk + 1) * CHUNK)
         value = feat8[:, here]
         sums = [
@@ -558,14 +622,14 @@
                 sums[:, b * 256 : b * 256 + 128],
                 turn_rows(sums[:, b * 256 + 128 : b * 256 + 256]),
             )
-    for r in range(GROUP - 1, 0, -1):
-        send(
-            tx_force.at[r],
-            rx_force.at[r - 1],
-            send_sem.at[9],
-            recv_sem.at[9],
-            at(*ring_back(RING[r])),
-        )
+        for r in range((chunk + 1) * blocks - 1, max(chunk * blocks, 1) - 1, -1):
+            send(
+                tx_force.at[r],
+                rx_force.at[r - 1],
+                send_sem.at[9],
+                recv_sem.at[9],
+                at(*ring_back(RING[r])),
+            )
     wait(ghost_in, recv_sem.at[6])
     rest = short_force[0] + jnp.concatenate([ghost_in[0], ghost_in[1]], 1)
     wait(rx_force, recv_sem.at[9])
@@ -587,9 +651,24 @@
     wait(tx_force.at[pl.ds(0, GROUP - 1)], send_sem.at[9])
 
 
+def hand_over(upd_ref, force_ref, upd_out, force_out, sem):
+    copies = [
+        pltpu.make_async_copy(upd_ref, upd_out, sem.at[0]),
+        pltpu.make_async_copy(force_ref, force_out, sem.at[1]),
+    ]
+    for copy in copies:
+        copy.start()
+    for copy in copies:
+        copy.wait()
+
+
 def on_device(positions, features, neighbours, miller, filter_weights, energy_weights):
     vmem = pl.BlockSpec(memory_space=pltpu.VMEM)
-    scratch = [
+    hbm = pl.BlockSpec(memory_space=pltpu.HBM)
+    filters = filter_weights.T
+    energy = energy_weights.reshape(1, 64)
+    inputs = (positions, features, neighbours, miller, filters, energy)
+    scratch = [(value.shape, value.dtype) for value in inputs] + [
         ((GROUP * 8, ATOMS_DEV), F32),
         ((8, WIDE), F32),
         ((72, 512), F32),
@@ -616,24 +695,32 @@
         ((2, 8, 128), F32),
         ((2, 8, 128), F32),
     ]
-    return pl.pallas_call(
+    found = pl.pallas_call(
         kernel,
         out_shape=(
             jax.ShapeDtypeStruct((64, ATOMS_DEV), F32),
             jax.ShapeDtypeStruct((3, ATOMS_DEV), F32),
         ),
-        in_specs=[vmem] * 6,
+        in_specs=[hbm] * 6,
         out_specs=(vmem, vmem),
         scratch_shapes=[pltpu.VMEM(shape, kind) for shape, kind in scratch]
         + [
             pltpu.SemaphoreType.DMA((len(ARRIVALS),)),
             pltpu.SemaphoreType.DMA((10,)),
             pltpu.SemaphoreType.DMA((10,)),
+            pltpu.SemaphoreType.DMA((len(inputs),)),
         ],
         compiler_params=pltpu.CompilerParams(
-            collective_id=0, has_side_effects=True, vmem_limit_bytes=40 * 2**20
+            collective_id=0, has_side_effects=True, vmem_limit_bytes=60 * 2**20
         ),
-    )(positions, features, neighbours, miller, filter_weights, energy_weights.reshape(1, 64))
+    )(*inputs)
+    return pl.pallas_call(
+        hand_over,
+        out_shape=tuple(jax.ShapeDtypeStruct(value.shape, F32) for value in found),
+        in_specs=[vmem] * 2,
+        out_specs=(hbm, hbm),
+        scratch_shapes=[pltpu.SemaphoreType.DMA((2,))],
+    )(*found)
 
 
 def solution(mesh):

time: 50.4 us -> 48.6 us (0.964)
  local copies, waits for them, and re-layouts: 2.64 us -> 0 us
  Pallas kernels: 46.9 us -> 47.8 us
    unnamed x13 -> x0, local copies, waits for them, and re-layouts: 2.64 us -> none
    pallas_call x0 -> x1, Pallas kernels: none -> 1.49 us  [on_device(): pl.pallas_call(hand_over, out_shape=tuple((jax.ShapeDtypeStruct(value.sha...]
    pallas_call x1, Pallas kernels: 46.9 us -> 46.3 us  [on_device(): pl.pallas_call(kernel, out_shape=(jax.ShapeDtypeStruct((64, ATOMS_DEV), F...]
where the time goes in v2:
time: 48.6 us; the launch traced here: 48.4 us
  Pallas kernels  47.8 us (98%)
  between operations  0.64 us (1%)
    pallas_call x1, Pallas kernels, on_device(): pl.pallas_call(kernel, out_shape=(jax.ShapeDtypeStruct((64, ATOMS_DEV), F...  46.3 us
    pallas_call x1, Pallas kernels, on_device(): pl.pallas_call(hand_over, out_shape=tuple((jax.ShapeDtypeStruct(value.sha...  1.49 us

profile of v2, /device:TPU:1, one launch (start us, length us, event | category | flops | bytes accessed | tf_op | source)
XLA Modules:
  0.0 48.4 jit_solution(16323204423037919776)
XLA Ops:
  0.6 46.3 %shard_map.77 = (f32[64,256]{1,0:T(8,128)}, f32[3,256]{1,0:T(4,128)}) custom-call(f32[3,256]{1,0:T(4,128)} %pos_hbm.1, bf16[64,256]{1,0:T(8,128)(2,1)} %feat_hbm.1, s32[16,256]{1,0:T(8,128)} %near_hbm.1, s32[3,2048]{1,0:T(4,128)} %miller_hbm.1, f32[64,2048]{1,0:T(8,128)} %bitcast.2, f32[1,64]{1,0:T(1,128)} %bitcast.3), custom_call_target="tpu_custom_call" | custom-call | tf_op jit(solution)/shard_map/pallas_call | solution.py:698
  46.9 1.5 %shard_map.78 = (f32[64,256]{1,0:T(8,128)}, f32[3,256]{1,0:T(4,128)}) custom-call(f32[64,256]{1,0:T(8,128)} %get-tuple-element.4.upd_ref, f32[3,256]{1,0:T(4,128)} %get-tuple-element.5.force_ref), custom_call_target="tpu_custom_call" | custom-call | tf_op jit(solution)/shard_map/pallas_call | solution.py:717

commit v3 on v2

--- a/solution.py
+++ b/solution.py
@@ -20,15 +20,15 @@
 NBR = 16
 HALF = 40
 USED = 2 * HALF + 1
-GROUP = NZ * NC
+GROUP = NY * NC
 WIDE = GROUP * ATOMS_DEV
 CHUNK = 1024
 
 RING = sorted(
-    [(dz, dc) for dz in range(NZ) for dc in range(NC)],
-    key=lambda o: (min(o[0], NZ - o[0]), o[0], o[1]),
+    [(dy, dc) for dy in range(NY) for dc in range(NC)],
+    key=lambda o: (min(o[0], NY - o[0]), o[0], o[1]),
 )
-FAR_Y = (4, 3, 5, 2, 6, 1, 7)
+FAR_Z = (4, 3, 5, 2, 6, 1, 7)
 FAR_X = (2, 1, 3)
 ARRIVALS = ((0, 2), (2, 6), (6, 10), (10, 14), (14, 16))
 
@@ -214,9 +214,9 @@
     grad8,
     slopes,
     pairs,
-    y1,
+    z1,
     x1,
-    y2,
+    z2,
     x2,
     part1,
     part1x,
@@ -244,17 +244,17 @@
     core = lax.rem(sub, 2)
     x = x_hi * 2 + x_lo
 
-    def at(zz, cc):
-        return {"slab": x_lo * NZ + zz, "sub": y * 4 + x_hi * 2 + cc}
+    def at(yy, cc):
+        return {"slab": slab, "sub": yy * 4 + x_hi * 2 + cc}
 
     def ring(off):
-        return lax.rem(z + off[0], NZ), lax.rem(core + off[1], NC)
+        return lax.rem(y + off[0], NY), lax.rem(core + off[1], NC)
 
     def ring_back(off):
-        return lax.rem(z + NZ - off[0], NZ), lax.rem(core + off[1], NC)
-
-    def along_y(d):
-        return {"slab": slab, "sub": lax.rem(y + d, NY) * 4 + x_hi * 2 + core}
+        return lax.rem(y + NY - off[0], NY), lax.rem(core + off[1], NC)
+
+    def along_z(d):
+        return {"slab": x_lo * NZ + lax.rem(z + d, NZ), "sub": sub}
 
     def along_x(d):
         xx = lax.rem(x + d, NX)
@@ -294,7 +294,7 @@
 
     barrier = pltpu.get_barrier_semaphore()
     greeted = [at(*ring(off)) for off in RING[:0:-1]]
-    greeted += [along_y(d) for d in FAR_Y]
+    greeted += [along_z(d) for d in FAR_Z]
     greeted += [along_x(d) for d in FAR_X]
     greeted += [upper, lower]
     for device in greeted:
@@ -316,31 +316,31 @@
     ext[0:64, 128:384] = feats
     ext[64:72, 128:384] = place
     place4 = turn_rows(place)
-    for m in range(NZ):
+    for m in range(NY):
         rows = feats[8 * m : 8 * m + 8]
         tx1[16 * m : 16 * m + 8] = jnp.where(first4, rows, place4)
         tx1[16 * m + 8 : 16 * m + 16] = jnp.where(first4, turn_rows(rows), place4)
-    own = z * NC + core
+    own = y * NC + core
     rx1[:, 0:ATOMS_DEV] = tx1[pl.ds(pl.multiple_of(own * 8, 8), 8)]
 
     pl.semaphore_wait(barrier, len(greeted))
 
     for r in range(GROUP - 1, 0, -1):
-        zz, cc = ring(RING[r])
+        yy, cc = ring(RING[r])
         group = [g for g, (lo, hi) in enumerate(ARRIVALS) if lo <= r < hi][0]
         send(
-            tx1.at[pl.ds(pl.multiple_of((zz * NC + cc) * 8, 8), 8)],
+            tx1.at[pl.ds(pl.multiple_of((yy * NC + cc) * 8, 8), 8)],
             rx1.at[:, pl.ds(r * ATOMS_DEV, ATOMS_DEV)],
             send_sem.at[0],
             first_sem.at[group],
-            at(zz, cc),
+            at(yy, cc),
         )
     send(ext.at[:, pl.ds(256, 128)], ext.at[:, pl.ds(0, 128)], send_sem.at[1], recv_sem.at[1], upper)
     send(ext.at[:, pl.ds(128, 128)], ext.at[:, pl.ds(384, 128)], send_sem.at[1], recv_sem.at[1], lower)
 
     for load in loads[2:]:
         load.wait()
-    channel = 8 * z + 4 * core
+    channel = 8 * y + 4 * core
     pick = jnp.where(
         lanes_like((8, 64)) == channel + lax.rem(rows_like((8, 64)), 4), 1.0, 0.0
     )
@@ -407,14 +407,14 @@
         total = total + dot(stacked_halves(modes), basis[:, here], (1, 1))
     own_modes = total[0:40, 0:128] + total[0:40, 128:256] + total[40:80, 0:128]
 
-    def add_y(own_part, src, buf, index, later):
+    def add_z(own_part, src, buf, index, later):
         src[...] = own_part
-        for d in FAR_Y:
-            send(src, buf.at[d - 1], send_sem.at[index], recv_sem.at[index], along_y(d))
+        for d in FAR_Z:
+            send(src, buf.at[d - 1], send_sem.at[index], recv_sem.at[index], along_z(d))
         later()
         wait(buf, recv_sem.at[index])
         out = src[...]
-        for d in range(NY - 1):
+        for d in range(NZ - 1):
             out = out + buf[d]
         return out
 
@@ -451,16 +451,16 @@
         high, low = halves(weights)
         ext_feat = ext[0:64].astype(BF16)
         short = 0.25 * (dot(ext_feat, high.astype(BF16)) + dot(ext_feat, low.astype(BF16)))
-        for m in range(NZ):
+        for m in range(NY):
             rows = short[8 * m : 8 * m + 8]
             turned = turn_rows(rows)
             tx_short[2 * m] = jnp.where(tile_row < 4, rows[:, 0:128], turned[:, 128:256])
             tx_short[2 * m + 1] = jnp.where(tile_row < 4, turned[:, 0:128], rows[:, 128:256])
         rx_short[0] = tx_short[own]
         for r in range(GROUP - 1, 0, -1):
-            zz, cc = ring(RING[r])
+            yy, cc = ring(RING[r])
             send(
-                tx_short.at[zz * NC + cc], rx_short.at[r], send_sem.at[2], recv_sem.at[2], at(zz, cc)
+                tx_short.at[yy * NC + cc], rx_short.at[r], send_sem.at[2], recv_sem.at[2], at(yy, cc)
             )
 
     held_filters = []
@@ -501,7 +501,7 @@
             scale * jnp.concatenate([summed[:, 0:128], summed[0:16, 128:256]], 0)
         )
 
-    part = add_y(pack_modes(own_modes), part1, y1, 3, short_values)
+    part = add_z(pack_modes(own_modes), part1, z1, 3, short_values)
     factor = add_x(part, part1x, x1, 4, add_filters)
     filters = held_filters[0]
     weighted = weigh(factor, filters)
@@ -563,8 +563,8 @@
     def first_slopes():
         rx_upd[own] = tx_upd[0]
         for r in range(GROUP - 1, 0, -1):
-            zz, cc = ring_back(RING[r])
-            send(tx_upd.at[r], rx_upd.at[own], send_sem.at[5], recv_sem.at[5], at(zz, cc))
+            yy, cc = ring_back(RING[r])
+            send(tx_upd.at[r], rx_upd.at[own], send_sem.at[5], recv_sem.at[5], at(yy, cc))
         slope_operand = left_operand(with_slopes(weighted))
         for chunk in range(WIDE // CHUNK):
             here = slice(chunk * CHUNK, (chunk + 1) * CHUNK)
@@ -577,7 +577,7 @@
     def short_forces():
         others = rx_upd.at[pl.ds(0, GROUP - 1)]
         wait(others, recv_sem.at[5])
-        for m in range(NZ):
+        for m in range(NY):
             low, high = rx_upd[2 * m], rx_upd[2 * m + 1]
             upd_ref[8 * m : 8 * m + 8, 0:128] = jnp.where(tile_row < 4, low, turn_rows(high))
             upd_ref[8 * m : 8 * m + 8, 128:256] = jnp.where(tile_row < 4, turn_rows(low), high)
@@ -605,7 +605,7 @@
         send(ghost_out.at[1], ghost_in.at[0], send_sem.at[6], recv_sem.at[6], upper)
         short_force.append(mine_acc + ext_acc[:, 128:384])
 
-    part = add_y(pack_modes(own_modes), part2, y2, 7, first_slopes)
+    part = add_z(pack_modes(own_modes), part2, z2, 7, first_slopes)
     factor = add_x(part, part2x, x2, 8, short_forces)
     slope_operand = left_operand(with_slopes(weigh(factor, filters)))
     for chunk in range(WIDE // CHUNK - 1, -1, -1):
@@ -642,11 +642,11 @@
     wait(tx1.at[pl.ds(0, 8 * (GROUP - 1))], send_sem.at[0])
     wait(ext.at[:, pl.ds(0, 256)], send_sem.at[1])
     wait(tx_short.at[pl.ds(0, GROUP - 1)], send_sem.at[2])
-    wait(y1, send_sem.at[3])
+    wait(z1, send_sem.at[3])
     wait(x1, send_sem.at[4])
     wait(tx_upd.at[pl.ds(0, GROUP - 1)], send_sem.at[5])
     wait(ghost_out, send_sem.at[6])
-    wait(y2, send_sem.at[7])
+    wait(z2, send_sem.at[7])
     wait(x2, send_sem.at[8])
     wait(tx_force.at[pl.ds(0, GROUP - 1)], send_sem.at[9])
 
@@ -678,9 +678,9 @@
         ((8, WIDE), F32),
         ((24, WIDE), F32),
         ((512, ATOMS_DEV), F32),
-        ((NY - 1, 24, 128), F32),
+        ((NZ - 1, 24, 128), F32),
         ((NX - 1, 24, 128), F32),
-        ((NY - 1, 24, 128), F32),
+        ((NZ - 1, 24, 128), F32),
         ((NX - 1, 24, 128), F32),
         ((24, 128), F32),
         ((24, 128), F32),

time: 48.6 us -> 48.4 us (level)
  no operation moved by 1% of the time
where the time goes in v3:
time: 48.4 us; the launch traced here: 48.2 us
  Pallas kernels  47.6 us (98%)
  between operations  0.64 us (1%)
    pallas_call x1, Pallas kernels, on_device(): pl.pallas_call(kernel, out_shape=(jax.ShapeDtypeStruct((64, ATOMS_DEV), F...  46.1 us
    pallas_call x1, Pallas kernels, on_device(): pl.pallas_call(hand_over, out_shape=tuple((jax.ShapeDtypeStruct(value.sha...  1.49 us

profile of v3, /device:TPU:1, one launch (start us, length us, event | category | flops | bytes accessed | tf_op | source)
XLA Modules:
  0.0 48.2 jit_solution(6998194846973005264)
XLA Ops:
  0.6 46.1 %shard_map.77 = (f32[64,256]{1,0:T(8,128)}, f32[3,256]{1,0:T(4,128)}) custom-call(f32[3,256]{1,0:T(4,128)} %pos_hbm.1, bf16[64,256]{1,0:T(8,128)(2,1)} %feat_hbm.1, s32[16,256]{1,0:T(8,128)} %near_hbm.1, s32[3,2048]{1,0:T(4,128)} %miller_hbm.1, f32[64,2048]{1,0:T(8,128)} %bitcast.2, f32[1,64]{1,0:T(1,128)} %bitcast.3), custom_call_target="tpu_custom_call" | custom-call | tf_op jit(solution)/shard_map/pallas_call | solution.py:698
  46.7 1.5 %shard_map.78 = (f32[64,256]{1,0:T(8,128)}, f32[3,256]{1,0:T(4,128)}) custom-call(f32[64,256]{1,0:T(8,128)} %get-tuple-element.4.upd_ref, f32[3,256]{1,0:T(4,128)} %get-tuple-element.5.force_ref), custom_call_target="tpu_custom_call" | custom-call | tf_op jit(solution)/shard_map/pallas_call | solution.py:717

commit v4 on v3

--- a/solution.py
+++ b/solution.py
@@ -22,7 +22,8 @@
 USED = 2 * HALF + 1
 GROUP = NY * NC
 WIDE = GROUP * ATOMS_DEV
-CHUNK = 1024
+CHUNK = 512
+FORCE_CHUNK = 512
 
 RING = sorted(
     [(dy, dc) for dy in range(NY) for dc in range(NC)],
@@ -30,7 +31,7 @@
 )
 FAR_Z = (4, 3, 5, 2, 6, 1, 7)
 FAR_X = (2, 1, 3)
-ARRIVALS = ((0, 2), (2, 6), (6, 10), (10, 14), (14, 16))
+ARRIVALS = ((0, 1), (1, 2), (2, 6), (6, 10), (10, 14), (14, 16))
 
 
 def wave_coefficients():
@@ -323,50 +324,9 @@
     own = y * NC + core
     rx1[:, 0:ATOMS_DEV] = tx1[pl.ds(pl.multiple_of(own * 8, 8), 8)]
 
-    pl.semaphore_wait(barrier, len(greeted))
-
-    for r in range(GROUP - 1, 0, -1):
-        yy, cc = ring(RING[r])
-        group = [g for g, (lo, hi) in enumerate(ARRIVALS) if lo <= r < hi][0]
-        send(
-            tx1.at[pl.ds(pl.multiple_of((yy * NC + cc) * 8, 8), 8)],
-            rx1.at[:, pl.ds(r * ATOMS_DEV, ATOMS_DEV)],
-            send_sem.at[0],
-            first_sem.at[group],
-            at(yy, cc),
-        )
-    send(ext.at[:, pl.ds(256, 128)], ext.at[:, pl.ds(0, 128)], send_sem.at[1], recv_sem.at[1], upper)
-    send(ext.at[:, pl.ds(128, 128)], ext.at[:, pl.ds(384, 128)], send_sem.at[1], recv_sem.at[1], lower)
-
-    for load in loads[2:]:
-        load.wait()
-    channel = 8 * y + 4 * core
-    pick = jnp.where(
-        lanes_like((8, 64)) == channel + lax.rem(rows_like((8, 64)), 4), 1.0, 0.0
-    )
-    energy_row = energy_ref[...]
-    energy8 = jnp.sum(pick * energy_row, 1, keepdims=True)
-    energy64 = jnp.sum(
-        jnp.where(rows_like((64, 64)) == lanes_like((64, 64)), energy_row, 0.0),
-        1,
-        keepdims=True,
-    )
-
-    near = near_ref[...]
-    ext_row = rows_like((ATOMS_DEV + 2 * GHOST, ATOMS_DEV))
-    count = jnp.zeros(ext_row.shape, F32)
-    for n in range(NBR):
-        count = count + jnp.where(ext_row == near[n : n + 1, :], 1.0, 0.0)
-    pairs[0:64] = jnp.zeros((64, ATOMS_DEV), F32)
-    pairs[448:512] = jnp.zeros((64, ATOMS_DEV), F32)
-    pairs[64:448] = count
-
-    total = jnp.zeros((80, 256), F32)
-    for group, (lo, hi) in enumerate(ARRIVALS):
+    def block_modes(lo, hi):
         width = (hi - lo) * ATOMS_DEV
         here = slice(lo * ATOMS_DEV, hi * ATOMS_DEV)
-        recv = rx1.at[:, pl.ds(max(lo, 1) * ATOMS_DEV, (hi - max(lo, 1)) * ATOMS_DEV)]
-        wait(recv, first_sem.at[group])
         block = rx1[:, here]
         row = rows_like((8, width))
         upper_half = row < 4
@@ -404,7 +364,54 @@
         value = jnp.where(upper_half, block, turn_rows(block))
         feat8[:, here] = value
         modes = jnp.concatenate([value * wave for wave in waves_x] + [value], 0)
-        total = total + dot(stacked_halves(modes), basis[:, here], (1, 1))
+        return dot(stacked_halves(modes), basis[:, here], (1, 1))
+
+    total = block_modes(0, 1)
+
+    loads[5].wait()
+    near = near_ref[...]
+    ext_row = rows_like((ATOMS_DEV + 2 * GHOST, ATOMS_DEV))
+    count = jnp.zeros(ext_row.shape, F32)
+    for n in range(NBR):
+        count = count + jnp.where(ext_row == near[n : n + 1, :], 1.0, 0.0)
+    pairs[0:64] = jnp.zeros((64, ATOMS_DEV), F32)
+    pairs[448:512] = jnp.zeros((64, ATOMS_DEV), F32)
+    pairs[64:448] = count
+
+    pl.semaphore_wait(barrier, len(greeted))
+
+    for r in range(GROUP - 1, 0, -1):
+        yy, cc = ring(RING[r])
+        group = [g for g, (lo, hi) in enumerate(ARRIVALS) if lo <= r < hi][0]
+        send(
+            tx1.at[pl.ds(pl.multiple_of((yy * NC + cc) * 8, 8), 8)],
+            rx1.at[:, pl.ds(r * ATOMS_DEV, ATOMS_DEV)],
+            send_sem.at[0],
+            first_sem.at[group],
+            at(yy, cc),
+        )
+    send(ext.at[:, pl.ds(256, 128)], ext.at[:, pl.ds(0, 128)], send_sem.at[1], recv_sem.at[1], upper)
+    send(ext.at[:, pl.ds(128, 128)], ext.at[:, pl.ds(384, 128)], send_sem.at[1], recv_sem.at[1], lower)
+
+    for load in loads[2:5]:
+        load.wait()
+    channel = 8 * y + 4 * core
+    pick = jnp.where(
+        lanes_like((8, 64)) == channel + lax.rem(rows_like((8, 64)), 4), 1.0, 0.0
+    )
+    energy_row = energy_ref[...]
+    energy8 = jnp.sum(pick * energy_row, 1, keepdims=True)
+    energy64 = jnp.sum(
+        jnp.where(rows_like((64, 64)) == lanes_like((64, 64)), energy_row, 0.0),
+        1,
+        keepdims=True,
+    )
+
+    for group, (lo, hi) in enumerate(ARRIVALS):
+        if lo == 0:
+            continue
+        wait(rx1.at[:, pl.ds(lo * ATOMS_DEV, (hi - lo) * ATOMS_DEV)], first_sem.at[group])
+        total = total + block_modes(lo, hi)
     own_modes = total[0:40, 0:128] + total[0:40, 128:256] + total[40:80, 0:128]
 
     def add_z(own_part, src, buf, index, later):
@@ -541,7 +548,7 @@
         total = total + dot(stacked_halves(modes), basis[:, here], (1, 1))
     own_modes = total[0:40, 0:128] + total[0:40, 128:256] + total[40:80, 0:128]
 
-    order12 = (TWO_PI * (1 + rows_like((8, CHUNK)) // 4)).astype(F32)
+    order12 = (TWO_PI * (1 + rows_like((8, 128)) // 4)).astype(F32)[:, 0:1]
     order34 = order12 + 2.0 * TWO_PI
 
     def field_slopes(slope_operand, here):
@@ -608,21 +615,22 @@
     part = add_z(pack_modes(own_modes), part2, z2, 7, first_slopes)
     factor = add_x(part, part2x, x2, 8, short_forces)
     slope_operand = left_operand(with_slopes(weigh(factor, filters)))
-    for chunk in range(WIDE // CHUNK - 1, -1, -1):
-        here = slice(chunk * CHUNK, (chunk + 1) * CHUNK)
+    force_blocks = FORCE_CHUNK // ATOMS_DEV
+    for chunk in range(WIDE // FORCE_CHUNK - 1, -1, -1):
+        here = slice(chunk * FORCE_CHUNK, (chunk + 1) * FORCE_CHUNK)
         value = feat8[:, here]
         sums = [
             jnp.sum(slopes[8 * d : 8 * d + 8, here] + value * along, 0, keepdims=True)
             for d, along in enumerate(field_slopes(slope_operand, here))
         ]
-        sums = jnp.concatenate(sums + [jnp.zeros((5, CHUNK), F32)], 0)
-        for b in range(blocks):
-            tx_force[chunk * blocks + b] = jnp.where(
+        sums = jnp.concatenate(sums + [jnp.zeros((5, FORCE_CHUNK), F32)], 0)
+        for b in range(force_blocks):
+            tx_force[chunk * force_blocks + b] = jnp.where(
                 tile_row < 4,
                 sums[:, b * 256 : b * 256 + 128],
                 turn_rows(sums[:, b * 256 + 128 : b * 256 + 256]),
             )
-        for r in range((chunk + 1) * blocks - 1, max(chunk * blocks, 1) - 1, -1):
+        for r in range((chunk + 1) * force_blocks - 1, max(chunk * force_blocks, 1) - 1, -1):
             send(
                 tx_force.at[r],
                 rx_force.at[r - 1],

time: 48.4 us -> 48 us (level)
  Pallas kernels: 47.6 us -> 47.1 us
where the time goes in v4:
time: 48 us; the launch traced here: 47.8 us
  Pallas kernels  47.1 us (98%)
  between operations  0.64 us (1%)
    pallas_call x1, Pallas kernels, on_device(): pl.pallas_call(kernel, out_shape=(jax.ShapeDtypeStruct((64, ATOMS_DEV), F...  45.6 us
    pallas_call x1, Pallas kernels, on_device(): pl.pallas_call(hand_over, out_shape=tuple((jax.ShapeDtypeStruct(value.sha...  1.49 us

profile of v4, /device:TPU:1, one launch (start us, length us, event | category | flops | bytes accessed | tf_op | source)
XLA Modules:
  0.0 47.8 jit_solution(13229606600325544141)
XLA Ops:
  0.6 45.6 %shard_map.77 = (f32[64,256]{1,0:T(8,128)}, f32[3,256]{1,0:T(4,128)}) custom-call(f32[3,256]{1,0:T(4,128)} %pos_hbm.1, bf16[64,256]{1,0:T(8,128)(2,1)} %feat_hbm.1, s32[16,256]{1,0:T(8,128)} %near_hbm.1, s32[3,2048]{1,0:T(4,128)} %miller_hbm.1, f32[64,2048]{1,0:T(8,128)} %bitcast.2, f32[1,64]{1,0:T(1,128)} %bitcast.3), custom_call_target="tpu_custom_call" | custom-call | tf_op jit(solution)/shard_map/pallas_call | solution.py:706
  46.3 1.5 %shard_map.78 = (f32[64,256]{1,0:T(8,128)}, f32[3,256]{1,0:T(4,128)}) custom-call(f32[64,256]{1,0:T(8,128)} %get-tuple-element.4.upd_ref, f32[3,256]{1,0:T(4,128)} %get-tuple-element.5.force_ref), custom_call_target="tpu_custom_call" | custom-call | tf_op jit(solution)/shard_map/pallas_call | solution.py:725

commit v5 on v4

--- a/solution.py
+++ b/solution.py
@@ -22,7 +22,7 @@
 USED = 2 * HALF + 1
 GROUP = NY * NC
 WIDE = GROUP * ATOMS_DEV
-CHUNK = 512
+CHUNK = 256
 FORCE_CHUNK = 512
 
 RING = sorted(

time: 48 us -> 48.1 us (level)
  no operation moved by 1% of the time
where the time goes in v5:
time: 48.1 us; the launch traced here: 47.8 us
  Pallas kernels  47.2 us (98%)
  between operations  0.64 us (1%)
    pallas_call x1, Pallas kernels, on_device(): pl.pallas_call(kernel, out_shape=(jax.ShapeDtypeStruct((64, ATOMS_DEV), F...  45.7 us
    pallas_call x1, Pallas kernels, on_device(): pl.pallas_call(hand_over, out_shape=tuple((jax.ShapeDtypeStruct(value.sha...  1.49 us

profile of v5, /device:TPU:1, one launch (start us, length us, event | category | flops | bytes accessed | tf_op | source)
XLA Modules:
  0.0 47.8 jit_solution(3383309667410587449)
XLA Ops:
  0.6 45.7 %shard_map.77 = (f32[64,256]{1,0:T(8,128)}, f32[3,256]{1,0:T(4,128)}) custom-call(f32[3,256]{1,0:T(4,128)} %pos_hbm.1, bf16[64,256]{1,0:T(8,128)(2,1)} %feat_hbm.1, s32[16,256]{1,0:T(8,128)} %near_hbm.1, s32[3,2048]{1,0:T(4,128)} %miller_hbm.1, f32[64,2048]{1,0:T(8,128)} %bitcast.2, f32[1,64]{1,0:T(1,128)} %bitcast.3), custom_call_target="tpu_custom_call" | custom-call | tf_op jit(solution)/shard_map/pallas_call | solution.py:706
  46.4 1.5 %shard_map.78 = (f32[64,256]{1,0:T(8,128)}, f32[3,256]{1,0:T(4,128)}) custom-call(f32[64,256]{1,0:T(8,128)} %get-tuple-element.4.upd_ref, f32[3,256]{1,0:T(4,128)} %get-tuple-element.5.force_ref), custom_call_target="tpu_custom_call" | custom-call | tf_op jit(solution)/shard_map/pallas_call | solution.py:725
